TPU v7x, 256 devices: a whole 4x4x8 slice. The times are simulated.
256 devices in a mesh: row: 8 (over z_hi, x), col: 32 (over z_lo, y, core).
Axes of the slice: x: 4, y: 4, z: 8 (z_hi: 2, z_lo: 4; z = z_hi * 4 + z_lo), core: 2. Of those that a mesh axis runs over, the one named last changes fastest.
Arguments:
- amplitudes: bfloat16 [32768, 4096], P('col', 'row'), may hold values from -6 to 6
- amplitude_mask: int32 [256, 32], P('col', 'row'), may hold values 0 or 1
- integrals: bfloat16 [4096, 8192], P('col', 'row'), may hold values from -0.09375 to 0.09375
- integral_mask: int32 [32, 64], P('col', 'row'), may hold values 0 or 1
- residual_in: bfloat16 [32768, 8192], P('col', 'row'), may hold values from -6 to 6
- residual_mask: int32 [256, 64], P('col', 'row'), may hold values 0 or 1
Outputs:
- residual_out: float32 [32768, 8192], P('col', 'row')
All inputs are finite; a program needn't handle non-finite values. No bound on the sum of `amplitude_mask` or of `integral_mask` or of `residual_mask` on one device may be relied on, other than what follows from the above.
Results may differ from a plain program's by a relative error of at most 0.0003.
Values may be sent and summed in bfloat16 or wider, within the bound.
A program may use at most 64 MiB of HBM per device.

v0:
```python
import jax
import jax.numpy as jnp
from jax import lax
from jax.sharding import PartitionSpec as P

TILE = 128


def screen(values, tile_mask):
    above, across = tile_mask.shape
    blocks = values.reshape(above, TILE, across, TILE)
    factor = tile_mask.astype(values.dtype)[:, None, :, None]
    return (blocks * factor).reshape(values.shape)


def local(amplitudes, amplitude_mask, integrals, integral_mask, residual_in, residual_mask):
    screened_amplitudes = screen(amplitudes, amplitude_mask)
    screened_integrals = screen(integrals, integral_mask)
    integral_rows = lax.all_gather(screened_integrals, "col", axis=0, tiled=True)
    ladder = jnp.dot(
        lax.all_gather(screened_amplitudes, "row", axis=1, tiled=True),
        integral_rows,
        preferred_element_type=jnp.float32,
    )
    return residual_in.astype(jnp.float32) + screen(ladder, residual_mask)


def solution(mesh):
    placed = (
        P("col", "row"),
        P("col", "row"),
        P("col", "row"),
        P("col", "row"),
        P("col", "row"),
        P("col", "row"),
    )
    return jax.shard_map(
        local, mesh=mesh, in_specs=placed, out_specs=P("col", "row"), check_vma=False
    )
```

profile of v0, /device:TPU:6, one launch (start us, length us, event | category | flops | bytes accessed | tf_op | source)
XLA Modules:
  0.0 285.7 jit_solution(7816987960503310550)
XLA Ops:
  6.5 0.0 copy-start.3
  6.5 0.0 copy-start
  6.5 0.0 copy-start.1
  6.5 0.0 all-gather.3.cloned.1.call-start
  6.5 0.7 convert_element_type.13
  7.3 0.1 copy.7
  7.4 0.3 mul.39
  7.7 0.0 copy-start.2
  7.7 2.5 bitcast_multiply_fusion.1
  10.2 0.0 all-gather.3.cloned.1.call-update
  10.2 0.0 all-gather.5.cloned.1.call-start
  10.3 0.0 copy-done.3
  10.3 0.1 broadcast_bitcast_fusion
  10.4 0.0 copy-done
  10.4 0.7 broadcast_multiply_fusion
  11.1 0.0 all-gather.5.cloned.1.call-update
  11.1 0.0 copy-done.1
  11.2 184.7 %all-gather.3.cloned.1.call-done = bf16[1024,4096]{1,0:T(8,128)(2,1)} async-done(((bf16[1024,512]{1,0:T(8,128)(2,1)}), bf16[1024,4096]{1,0:T(8,128)(2,1)}) %all-gather.3.cloned.1.call-update) | async-done | bytes 8388624 | tf_op jit(solution)/shard_map/all_gather | solution.py:21
  195.8 66.9 %all-gather.5.cloned.1.call-done = bf16[4096,1024]{1,0:T(8,128)(2,1)} async-done(((bf16[128,1024]{1,0:T(8,128)(2,1)}), bf16[4096,1024]{1,0:T(8,128)(2,1)}) %all-gather.5.cloned.1.call-update) | async-done | bytes 8388624 | tf_op jit(solution)/shard_map/all_gather | solution.py:19
  262.8 0.3 mul.47
  263.1 0.0 copy-done.2
  263.1 15.8 %fusion = f32[1024,1024]{1,0:T(8,128)} fusion(f32[128,8,8,128]{3,2,1,0:T(8,128)S(1)} %bitcast.17, bf16[1024,1024]{1,0:T(8,128)(2,1)S(1)} %copy-done.2, bf16[1024,4096]{1,0:T(8,128)(2,1)} %all-gather.3.cloned.1.call-done, bf16[4096,1024]{1,0:T(8,128)(2,1)} %all-gather.5.cloned.1.call-done), kind=kOutput, calls=%fused_computation.1 | convolution fusion | flops 8593080320 | bytes 27262976 | tf_op jit(solution)/shard_map/dot_general | solution.py:20
  (2 shorter events, 0.0 us)
Async XLA Ops:
  6.5 3.8 %copy-start.3 = (s32[1,8]{1,0:T(1,128)S(1)}, s32[1,8]{1,0:T(1,128)}, u32[]{:S(2)}) copy-start(s32[1,8]{1,0:T(1,128)} %param.9) | copy-start | bytes 100
  6.5 3.9 %copy-start = (bf16[128,1024]{1,0:T(8,128)(2,1)S(1)}, bf16[128,1024]{1,0:T(8,128)(2,1)}, u32[]{:S(2)}) copy-start(bf16[128,1024]{1,0:T(8,128)(2,1)} %param.8) | copy-start | bytes 786436
  6.5 4.6 %copy-start.1 = (s32[8,8]{1,0:T(8,128)S(1)}, s32[8,8]{1,0:T(8,128)}, u32[]{:S(2)}) copy-start(s32[8,8]{1,0:T(8,128)} %param.11) | copy-start | bytes 772
  6.5 189.3 %all-gather.3.cloned.1.call-start = ((), (), s32[]{:S(2)}) async-start(), calls=%async_computation | async-start | bytes 9437184 | tf_op jit(solution)/shard_map/all_gather | solution.py:21
  7.7 255.4 %copy-start.2 = (bf16[1024,1024]{1,0:T(8,128)(2,1)S(1)}, bf16[1024,1024]{1,0:T(8,128)(2,1)}, u32[]{:S(2)}) copy-start(bf16[1024,1024]{1,0:T(8,128)(2,1)} %param.10) | copy-start | bytes 6291460
  10.2 252.5 %all-gather.5.cloned.1.call-start = ((), (), s32[]{:S(2)}) async-start(), calls=%async_computation.1 | async-start | bytes 8650752 | tf_op jit(solution)/shard_map/all_gather | solution.py:19
Sparse Core Ops, SparseCore 0:
  10.4 185.4 all-gather.2
  197.7 65.0 all-gather.4
where the time goes:
time: 287 us; the launch traced here: 286 us
  waiting for transfers between devices  252 us (88%)
  matrix products  15.8 us (6%)
  between operations  13.5 us (5%)
  other arithmetic  3.95 us (1%)
    all_gather x1, waiting for transfers between devices, local(): lax.all_gather(screened_amplitudes, 'row', axis=1, tiled=True)  185 us
    all_gather x1, waiting for transfers between devices, local(): lax.all_gather(screened_integrals, 'col', axis=0, tiled=True)  66.9 us
    dot_general x1, matrix products, local(): jnp.dot(lax.all_gather(screened_amplitudes, 'row', axis=1, tiled=True), i...  15.8 us
  transfers between devices with their start and end apart: 2, of which 2 were waited for; matrix products, arithmetic and copies ran while one was open for 0% of the time, Pallas kernels for 0%

commit v1 on v0

v1 whole, which is shorter than its diff:
```python
import functools

import jax
import jax.numpy as jnp
from jax import lax
from jax.experimental import pallas as pl
from jax.experimental.pallas import tpu as pltpu
from jax.sharding import PartitionSpec as P

MESH = pl.DeviceIdType.MESH
TILE = 128
XROWS = (128, 128, 128, 128)
ZROWS = (64, 64, 64, 64, 64, 64, 64, 64)
FIRST = 2
ZNEXT = 2
LAG = 2

ORDER = [
    ("xo", 1, 1, 0), ("xo", -1, -1, 0), ("xo", 1, 1, 1), ("xo", -1, -1, 1), ("vz", 1, 1), ("vz", -1, 1), ("vy", 1, 0),
    ("vy", -1, 0), ("z", 1, 1, 0), ("z", -1, 1, 0), ("xo", 1, 1, 2), ("xo", -1, -1, 2), ("z", 1, 1, 1),
    ("z", -1, 1, 1), ("xo", 1, 1, 3), ("xo", -1, -1, 3), ("vy", 1, -1), ("vy", -1, -1), ("vz", 1, 2), ("vz", -1, 2),
    ("z", 1, 2, 0), ("z", -1, 2, 0), ("z", 1, 2, 1), ("z", -1, 2, 1), ("vy", 1, 1), ("vy", -1, 1), ("vyf", 1, 0),
    ("vyf", -1, 0), ("vz", 1, 3), ("vz", -1, 3), ("z", 1, 3, 0), ("z", -1, 3, 0), ("vyf", 1, -1), ("vyf", -1, -1),
    ("z", 1, 1, 2), ("z", -1, 1, 2), ("z", 1, 3, 1), ("z", -1, 3, 1), ("z", 1, 1, 3), ("z", -1, 1, 3), ("vy", -1, -2),
    ("vy", 1, 2), ("vy", 1, -2), ("vy", -1, 2), ("z", 1, 4, 0), ("z", -1, 4, 0), ("vy", 1, -3), ("vy", -1, -3),
    ("vy", 1, 3), ("vy", -1, 3), ("z", 1, 2, 2), ("z", -1, 2, 2), ("vyf", 1, 1), ("vyf", -1, 1), ("z", -1, 4, 1),
    ("z", 1, 4, 1), ("z", -1, 2, 3), ("z", 1, 2, 3), ("po", 1, 1, 0), ("vyf", 1, 2), ("vyf", 1, -2), ("vyf", -1, 2),
    ("vyf", -1, -2), ("z", 1, 3, 2), ("z", -1, 3, 2), ("vyf", 1, 3), ("vyf", -1, -3), ("po", -1, -1, 0),
    ("vyf", 1, -3), ("vyf", -1, 3), ("z", 1, 1, 4), ("z", -1, 1, 4), ("po", -1, -1, 1), ("vk", 0, 0, 0),
    ("vk", 0, 0, -1), ("vk", 0, 0, 1), ("vk", 1, 1, 0), ("vk", 1, -1, 0), ("xo", 1, -1, 0), ("xo", -1, 1, 0),
    ("vk", 1, 1, -1), ("xo", 1, -1, 1), ("vk", 1, -1, -1), ("xo", -1, 1, 1), ("vk", 0, 0, -2), ("vk", 0, 0, 2),
    ("xo", 1, -1, 2), ("xo", -1, 1, 2), ("vk", 1, 1, 1), ("vk", 1, -1, 1), ("xo", 1, -1, 3), ("xo", -1, 1, 3),
    ("vk", 2, 1, 0), ("vk", 2, -1, 0), ("xf", 1, 1, 0), ("xf", -1, -1, 0), ("vk", 0, 0, -3), ("vk", 0, 0, 3),
    ("vk", 2, 1, -1), ("xf", 1, 1, 1), ("xf", -1, -1, 1), ("vk", 2, -1, -1), ("xf", 1, 1, 2), ("xf", -1, -1, 2),
    ("vk", 1, 1, 2), ("vk", 1, -1, -2), ("vk", 1, 1, -3), ("vk", 1, 1, 3), ("vk", 1, -1, 2), ("vk", 1, 1, -2),
    ("vk", 1, -1, -3), ("xf", 1, 1, 3), ("vk", 1, -1, 3), ("xf", -1, -1, 3), ("vk", 2, 1, 1), ("vk", 2, -1, 1),
    ("vk", 2, 1, 2), ("vk", 2, 1, -2), ("vk", 2, -1, 2), ("vk", 2, -1, -2), ("vk", 2, 1, 3), ("vk", 2, 1, -3),
    ("vk", 2, -1, -3), ("vk", 2, -1, 3), ("C", "oc", 0), ("po", 1, 1, 1), ("z", 1, 3, 3), ("z", -1, 3, 3),
    ("po", -1, 1, 0), ("po", -1, 1, 1), ("C", "p3", 0), ("z", 1, 1, 5), ("C", "oc", 1), ("z", -1, 1, 5),
    ("z", 1, 4, 2), ("z", -1, 4, 2), ("C", "oc", 2), ("pf", 1, 1, 0), ("pf", 1, 1, 1), ("C", "pl", 0), ("z", 1, 2, 4),
    ("z", -1, 2, 4), ("C", "oc", 3), ("C", "oc", 4), ("z", 1, 4, 3), ("po", 1, -1, 0), ("po", 1, -1, 1),
    ("C", "p3", 4), ("z", -1, 4, 3), ("pf", -1, -1, 0), ("pf", -1, -1, 1), ("C", "pl", 4), ("C", "oc", 5),
    ("z", 1, 2, 5), ("z", -1, 2, 5), ("C", "oc", 6), ("po", 1, 1, 2), ("po", -1, -1, 2), ("C", "oc", 7),
    ("z", 1, 3, 4), ("z", -1, 3, 4), ("z", 1, 1, 6), ("z", -1, 1, 6), ("po", 1, 1, 3), ("po", -1, 1, 2),
    ("po", -1, 1, 3), ("C", "p3", 1), ("po", 1, -1, 2), ("po", 1, -1, 3), ("po", -1, -1, 3), ("C", "p3", 5),
    ("z", 1, 3, 5), ("z", -1, 3, 5), ("z", 1, 1, 7), ("z", -1, 1, 7), ("z", 1, 4, 4), ("z", -1, 4, 4),
    ("pf", 1, 1, 2), ("pf", 1, 1, 3), ("C", "pl", 1), ("z", 1, 2, 6), ("z", -1, 2, 6), ("pf", -1, -1, 2),
    ("pf", -1, -1, 3), ("C", "pl", 5), ("z", 1, 4, 5), ("z", -1, 4, 5), ("po", 1, 1, 4), ("z", 1, 2, 7),
    ("z", -1, 2, 7), ("po", -1, -1, 4), ("z", 1, 3, 6), ("z", -1, 3, 6), ("po", 1, 1, 5), ("po", -1, 1, 4),
    ("po", -1, 1, 5), ("C", "p3", 2), ("z", 1, 3, 7), ("z", -1, 3, 7), ("po", 1, -1, 4), ("po", 1, -1, 5),
    ("po", -1, -1, 5), ("C", "p3", 6), ("z", 1, 4, 6), ("z", -1, 4, 6), ("pf", 1, 1, 4), ("pf", 1, 1, 5),
    ("C", "pl", 2), ("z", 1, 4, 7), ("pf", -1, -1, 4), ("pf", -1, -1, 5), ("C", "pl", 6), ("z", -1, 4, 7),
    ("po", 1, 1, 6), ("po", -1, -1, 6), ("po", 1, 1, 7), ("po", -1, 1, 6), ("po", -1, 1, 7), ("C", "p3", 3),
    ("po", 1, -1, 6), ("po", 1, -1, 7), ("po", -1, -1, 7), ("C", "p3", 7), ("pf", -1, -1, 6), ("pf", -1, -1, 7),
    ("C", "pl", 7), ("pf", 1, 1, 6), ("pf", 1, 1, 7), ("C", "pl", 3),
]


def starts():
    out = []
    for same in (1, -1):
        for i in range(len(XROWS)):
            for d in (1, -1):
                out.append((None, ("xo", d, same * d, i)))
    out += [(d, ("vz", d, 1)) for d in (1, -1)]
    out += [(None, ("z", d, 1, j)) for j in range(FIRST) for d in (1, -1)]
    out += [(None, ("vy", d, 0)) for d in (1, -1)]
    out.append((None, ("vk", 0, 0, 0)))
    return out


def follows(event):
    kind, out = event[0], []
    if kind == "xo":
        d, half, i = event[1:]
        if half == d:
            out.append((None, ("xf", d, d, i)))
    if kind == "z":
        d, h, j = event[1:]
        if h < 4:
            out.append((None, ("z", d, h + 1, j)))
        if h == ZNEXT and FIRST <= j + LAG < len(ZROWS):
            out.append((None, ("z", d, 1, j + LAG)))
        if h == 4:
            out += [(None, ("po", 1, d, j)), (None, ("po", -1, d, j))]
    if kind == "po":
        d, half, j = event[1:]
        if half == d:
            out.append((None, ("pf", d, d, j)))
    if kind == "vz":
        d, q = event[1:]
        if q < 3:
            out.append((d, ("vz", d, q + 1)))
        out += [(None, ("vy", 1, -d * q)), (None, ("vy", -1, -d * q))]
        out.append((None, ("vk", 0, 0, -d * q)))
    if kind == "vy":
        d, o = event[1:]
        out += [(None, ("vyf", d, o)), (None, ("vk", 1, d, o))]
    if kind == "vyf":
        d, o = event[1:]
        out.append((None, ("vk", 2, d, o)))
    return out


def offset(event):
    kind = event[0]
    if kind == "vz":
        return -event[1] * event[2]
    if kind in ("vy", "vyf"):
        return event[2]
    return event[3] if kind == "vk" else 0


def rows_of(half, pieces, i):
    return pl.ds((0 if half > 0 else 512) + sum(pieces[:i]), pieces[i])


SEMS = {
    "xo": (2, 2, len(XROWS)),
    "xf": (2, len(XROWS)),
    "z": (2, 4, len(ZROWS)),
    "po": (2, 2, len(ZROWS)),
    "pf": (2, len(ZROWS)),
    "vz": (2, 3),
    "vy": (2, 7),
    "vyf": (2, 7),
    "vk": (3, 2, 7),
}
KINDS = list(SEMS)


def sem_of(event):
    kind = event[0]
    way = lambda d: 0 if d > 0 else 1
    if kind in ("xo", "po"):
        return way(event[1]), way(event[2]), event[3]
    if kind in ("xf", "pf"):
        return way(event[1]), event[3]
    if kind == "z":
        return way(event[1]), event[2] - 1, event[3]
    if kind == "vz":
        return way(event[1]), event[2] - 1
    if kind in ("vy", "vyf"):
        return way(event[1]), event[2] + 3
    return event[1], way(event[2]), event[3] + 3


def kernel(a_in, v_in, res_in, a_mask, v_mask, r_mask, out, a, v, acc, res, relay, load_sem, out_sem, *sems):
    recv = dict(zip(KINDS, sems[: len(KINDS)]))
    sent = dict(zip(KINDS, sems[len(KINDS) :]))
    row, col = lax.axis_index("row"), lax.axis_index("col")
    zh, x = row // 4, row % 4
    zl, y, k = col // 8, (col // 2) % 4, col % 2
    z = 4 * zh + zl

    def at(dx=0, dy=0, dz=0, other=False):
        znew = (z + dz + 8) % 8
        return (
            4 * (znew // 4) + (x + dx + 4) % 4,
            8 * (znew % 4) + 2 * ((y + dy + 4) % 4) + (1 - k if other else k),
        )

    mine = lambda dx: 4 * zh + (x + dx + 4) % 4
    theirs = lambda dx: 4 * (1 - zh) + (x + dx + 4) % 4

    def v_rows(o, dy, half=0):
        start = (8 * (zl + o) + 2 * ((y + dy + 4) % 4) + k) * TILE
        if half == 0:
            return v.at[pl.ds(pl.multiple_of(start, TILE), TILE)]
        start = start + (0 if half > 0 else TILE // 2)
        return v.at[pl.ds(pl.multiple_of(start, TILE // 2), TILE // 2)]

    def copy(event):
        kind = event[0]
        if kind in ("xo", "xf", "po", "pf"):
            d, half, i = event[1:]
            slot = (mine if kind[0] == "x" else theirs)(0 if kind[1] == "o" else -d)
            src = dst = a.at[slot, rows_of(half, XROWS if kind[0] == "x" else ZROWS, i)]
            to = at(dx=d)
        elif kind == "z":
            d, h, j = event[1:]
            rows = rows_of(d, ZROWS, j)
            src = a.at[mine(0), rows] if h == 1 else relay.at[h - 2, rows]
            if h < 4:
                dst = relay.at[h - 1, rows]
            else:
                dst = a.at[4 * (1 - ((z + d + 8) % 8) // 4) + x, rows]
            to = at(dz=d)
        elif kind == "vz":
            d, q = event[1:]
            src = dst = v_rows(-d * (q - 1), 0)
            to = at(dz=d)
        elif kind == "vy":
            d, o = event[1:]
            src = dst = v_rows(o, 0)
            to = at(dy=d)
        elif kind == "vyf":
            d, o = event[1:]
            src = dst = v_rows(o, -d, d)
            to = at(dy=d)
        else:
            via, d, o = event[1:]
            src = dst = v_rows(o, -d * via, d if via == 2 else 0)
            to = at(other=True)
        return pltpu.make_async_remote_copy(
            src_ref=src,
            dst_ref=dst,
            send_sem=sent[kind].at[sem_of(event)],
            recv_sem=recv[kind].at[sem_of(event)],
            device_id=to,
            device_id_type=MESH,
        )

    def within(o, act):
        if o == 0:
            act()
        else:
            pl.when((zl + o >= 0) & (zl + o <= 3))(act)

    copies = []

    def send(step, event):
        copies.append((event, step))
        go = lambda: copy(event).start()
        if step is None:
            go()
        else:
            within(step, go)

    def arrive(event):
        def act():
            copy(event).wait_recv()
            for step, then in follows(event):
                here = lambda then=then: copy(then).start()
                if step is None:
                    here()
                else:
                    within(step, here)

        within(offset(event), act)
        copies.extend((then, (offset(event), step)) for step, then in follows(event))

    def product(slots, rows, cols):
        total = None
        for slot in slots:
            part = jnp.dot(
                a[slot, rows, :],
                v[pl.ds(pl.multiple_of(slot * 512, 512), 512), cols],
                preferred_element_type=jnp.float32,
            )
            total = part if total is None else total + part
        return total

    def multiply(which, c):
        rows = pl.ds(c * TILE, TILE)
        width = 512
        slots = {
            "oc": [mine(dx) for dx in (0, 1, 2, 3)],
            "p3": [theirs(dx) for dx in (0, 1, 3)],
            "pl": [theirs(2)],
        }[which]

        def columns(n, carry):
            cols = pl.ds(pl.multiple_of(n * width, width), width)
            total = product(slots, rows, cols)
            if which == "oc":
                acc[rows, cols] = total
            elif which == "p3":
                acc[rows, cols] += total
            else:
                total = total + acc[rows, cols]
                for t in range(width // TILE):
                    tile = pl.ds(pl.multiple_of(n * width + t * TILE, TILE), TILE)
                    keep = r_mask[c, n * (width // TILE) + t].astype(jnp.float32)
                    acc[rows, tile] = res[rows, tile].astype(jnp.float32) + keep * total[:, t * TILE : (t + 1) * TILE]
            return carry

        lax.fori_loop(0, 1024 // width, columns, 0)
        if which == "pl":
            pltpu.make_async_copy(acc.at[rows], out.at[rows], out_sem.at[c]).start()

    own_a = a.at[mine(0)]
    own_v = v_rows(0, 0)
    loads = [
        pltpu.make_async_copy(a_in, own_a, load_sem.at[0]),
        pltpu.make_async_copy(v_in, own_v, load_sem.at[1]),
        pltpu.make_async_copy(res_in, res, load_sem.at[2]),
    ]
    for load in loads:
        load.start()

    barrier = pltpu.get_barrier_semaphore()
    neighbours = [at(dx=1), at(dx=-1), at(dy=1), at(dy=-1), at(dz=1), at(dz=-1), at(other=True)]
    for neighbour in neighbours:
        pl.semaphore_signal(barrier, inc=1, device_id=neighbour, device_id_type=MESH)

    loads[0].wait()

    def screen_a(i, carry):
        rows = pl.ds(pl.multiple_of(i * TILE, TILE), TILE)
        for j in range(4):
            cols = pl.ds(j * TILE, TILE)
            keep = a_mask[i, j].astype(jnp.float32)
            a[mine(0), rows, cols] = (a[mine(0), rows, cols].astype(jnp.float32) * keep).astype(jnp.bfloat16)
        return carry

    lax.fori_loop(0, 8, screen_a, 0)
    loads[1].wait()
    own_rows = pl.ds(pl.multiple_of(col * TILE, TILE), TILE)
    for j in range(8):
        cols = pl.ds(j * TILE, TILE)
        keep = v_mask[0, j].astype(jnp.float32)
        v[own_rows, cols] = (v[own_rows, cols].astype(jnp.float32) * keep).astype(jnp.bfloat16)
    pl.semaphore_wait(barrier, len(neighbours))

    for step, event in starts():
        go = lambda event=event: copy(event).start()
        if step is None:
            go()
        else:
            within(step, go)
        copies.append((event, (0, step)))

    loads[2].wait()
    for op in ORDER:
        if op[0] == "C":
            multiply(op[1], op[2])
        else:
            arrive(op)

    for event, (o, step) in copies:
        def done(event=event, step=step):
            if step is None:
                copy(event).wait_send()
            else:
                within(step, lambda: copy(event).wait_send())

        within(o, done)
    for c in range(8):
        rows = pl.ds(c * TILE, TILE)
        pltpu.make_async_copy(acc.at[rows], out.at[rows], out_sem.at[c]).wait()


def local(amplitudes, amplitude_mask, integrals, integral_mask, residual_in, residual_mask):
    hbm = pl.BlockSpec(memory_space=pl.ANY)
    smem = pl.BlockSpec(memory_space=pltpu.SMEM)
    semaphores = [pltpu.SemaphoreType.DMA(shape) for shape in SEMS.values()]
    return pl.pallas_call(
        kernel,
        out_shape=jax.ShapeDtypeStruct((1024, 1024), jnp.float32),
        in_specs=[hbm, hbm, hbm, smem, smem, smem],
        out_specs=hbm,
        scratch_shapes=[
            pltpu.VMEM((8, 1024, 512), jnp.bfloat16),
            pltpu.VMEM((4096, 1024), jnp.bfloat16),
            pltpu.VMEM((1024, 1024), jnp.float32),
            pltpu.VMEM((1024, 1024), jnp.bfloat16),
            pltpu.VMEM((3, 1024, 512), jnp.bfloat16),
            pltpu.SemaphoreType.DMA((3,)),
            pltpu.SemaphoreType.DMA((8,)),
            *semaphores,
            *semaphores,
        ],
        compiler_params=pltpu.CompilerParams(
            collective_id=0, has_side_effects=True, vmem_limit_bytes=48 * 1024 * 1024
        ),
        cost_estimate=pl.CostEstimate(flops=2 * 1024 * 4096 * 1024, bytes_accessed=12 << 20, transcendentals=0),
        name="ladder",
    )(amplitudes, integrals, residual_in, amplitude_mask, integral_mask, residual_mask)


def solution(mesh):
    placed = P("col", "row")
    return jax.shard_map(
        local, mesh=mesh, in_specs=(placed,) * 6, out_specs=placed, check_vma=False
    )
```

time: 287 us -> 103 us (0.36)
  waiting for transfers between devices: 252 us -> 0 us
  Pallas kernels: 0 us -> 92.5 us
  matrix products: 15.8 us -> 0 us
  between operations: 13.5 us -> 0.01 us
  local copies, waits for them, and re-layouts: 0.86 us -> 10.6 us
  other arithmetic: 3.95 us -> 0 us
    all_gather x2 -> x0, waiting for transfers between devices: 252 us -> none  [the longest x1 185 us: local(): lax.all_gather(screened_amplitudes, 'row', axis=1, tiled=True)]
    pallas_call x0 -> x1, Pallas kernels: none -> 92.5 us  [local(): pl.pallas_call(kernel, out_shape=jax.ShapeDtypeStruct((1024, 1024), jnp.f...]
    dot_general x1 -> x0, matrix products: 15.8 us -> none  [local(): jnp.dot(lax.all_gather(screened_amplitudes, 'row', axis=1, tiled=True), i...]
    unnamed x8 -> x12, local copies, waits for them, and re-layouts: 0.02 us -> 10.6 us
    mul x3 -> x0, other arithmetic: 3.21 us -> none  [screen(): return (blocks * factor).reshape(values.shape)]
  transfers between devices with their start and end apart: 2 -> 0, of which waited for: 2 -> 0; matrix products, arithmetic and copies ran while one was open for 0% -> 0% of each run, Pallas kernels for 0% -> 0%
where the time goes in v1:
time: 103 us
  Pallas kernels  92.5 us (90%)
  local copies, waits for them, and re-layouts  10.6 us (10%)
    pallas_call x1, Pallas kernels, local(): pl.pallas_call(kernel, out_shape=jax.ShapeDtypeStruct((1024, 1024), jnp.f...  92.5 us
    unnamed x12, local copies, waits for them, and re-layouts  10.6 us

profile of v1, /device:TPU:6, one launch (start us, length us, event | category | flops | bytes accessed | tf_op | source)
XLA Modules:
  0.0 103.2 jit_solution(5288788671870249107)
XLA Ops:
  0.0 0.8 copy.7.a_mask
  0.8 0.0 copy-start
  0.8 1.6 %copy-done = bf16[1024,1024]{1,0:T(8,128)(2,1)S(1)} copy-done((bf16[1024,1024]{1,0:T(8,128)(2,1)S(1)}, bf16[1024,1024]{1,0:T(8,128)(2,1)}, u32[]{:S(2)}) %copy-start) | copy-done | bytes 2097176
  2.3 0.0 copy-start.1
  2.4 1.2 %copy-done.1 = bf16[1024,512]{1,0:T(8,128)(2,1)S(1)} copy-done((bf16[1024,512]{1,0:T(8,128)(2,1)S(1)}, bf16[1024,512]{1,0:T(8,128)(2,1)}, u32[]{:S(2)}) %copy-start.1) | copy-done | bytes 1048600
  3.6 0.0 copy-start.2
  3.6 0.9 copy-done.2
  4.5 0.0 copy-start.3
  4.5 0.7 copy-done.3
  5.2 0.0 copy-start.4
  5.2 0.7 copy-done.4
  5.9 92.5 %ladder.1 = f32[1024,1024]{1,0:T(8,128)} custom-call(bf16[1024,512]{1,0:T(8,128)(2,1)S(1)} %copy-done.1, bf16[128,1024]{1,0:T(8,128)(2,1)S(1)} %copy-done.2, bf16[1024,1024]{1,0:T(8,128)(2,1)S(1)} %copy-done, s32[8,4]{1,0:T(8,128)S(1)} %copy.7.a_mask, s32[1,8]{1,0:T(1,128)S(1)} %copy-done.4, s32[8,8]{1,0:T(8,128)S(1)} %copy-done.3), custom_call_target="tpu_custom_call" | custom-call | flops 8589934592 | bytes 12582912 | tf_op jit(solution)/shard_map/ladder/pallas_call | solution.py:348
  98.4 4.8 %copy.9 = f32[1024,1024]{1,0:T(8,128)} copy(f32[1024,1024]{1,0:T(8,128)} %ladder.1) | data formatting | bytes 8388608
Async XLA Ops:
  0.8 1.6 %copy-start = (bf16[1024,1024]{1,0:T(8,128)(2,1)S(1)}, bf16[1024,1024]{1,0:T(8,128)(2,1)}, u32[]{:S(2)}) copy-start(bf16[1024,1024]{1,0:T(8,128)(2,1)} %res_in.1) | copy-start | bytes 6291460
  2.3 1.2 %copy-start.1 = (bf16[1024,512]{1,0:T(8,128)(2,1)S(1)}, bf16[1024,512]{1,0:T(8,128)(2,1)}, u32[]{:S(2)}) copy-start(bf16[1024,512]{1,0:T(8,128)(2,1)} %a_in.1) | copy-start | bytes 3145732
  3.6 0.9 copy-start.2
  4.5 0.7 copy-start.3
  5.2 0.7 copy-start.4

commit v2 on v1

v2 whole, which is shorter than its diff:
```python
import functools

import jax
import jax.numpy as jnp
from jax import lax
from jax.experimental import pallas as pl
from jax.experimental.pallas import tpu as pltpu
from jax.sharding import PartitionSpec as P

MESH = pl.DeviceIdType.MESH
TILE = 128
XROWS = (128, 128, 128, 128)
ZROWS = (64, 64, 64, 64, 64, 64, 64, 64)
FIRST = 2
ZNEXT = 2
LAG = 2
ZSTEP = 1
HOPS = 4 // ZSTEP

MROWS = {"oc": 128, "p3": 128, "pl": 128}
NCOLS = {"oc": 512, "p3": 512, "pl": 1024}

ORDER = [
    ("xo", 1, 1, 0), ("xo", -1, -1, 0), ("xo", 1, 1, 1), ("xo", -1, -1, 1), ("vz", 1, 1), ("vz", -1, 1), ("vy", 1, 0),
    ("vy", -1, 0), ("z", 1, 1, 0), ("z", -1, 1, 0), ("xo", 1, 1, 2), ("xo", -1, -1, 2), ("z", 1, 1, 1),
    ("z", -1, 1, 1), ("xo", 1, 1, 3), ("xo", -1, -1, 3), ("vy", 1, -1), ("vy", -1, -1), ("vz", 1, 2), ("vz", -1, 2),
    ("z", 1, 2, 0), ("z", -1, 2, 0), ("z", 1, 2, 1), ("z", -1, 2, 1), ("vy", 1, 1), ("vy", -1, 1), ("vyf", 1, 0),
    ("vyf", -1, 0), ("vz", 1, 3), ("vz", -1, 3), ("z", 1, 3, 0), ("z", -1, 3, 0), ("vyf", 1, -1), ("vyf", -1, -1),
    ("z", 1, 1, 2), ("z", -1, 1, 2), ("z", 1, 3, 1), ("z", -1, 3, 1), ("z", 1, 1, 3), ("z", -1, 1, 3), ("z", 1, 4, 0),
    ("z", -1, 4, 0), ("vy", 1, 2), ("vy", 1, -2), ("vy", 1, -3), ("vy", -1, -2), ("vy", -1, 2), ("vy", -1, -3),
    ("vy", 1, 3), ("vy", -1, 3), ("z", 1, 2, 2), ("z", -1, 2, 2), ("z", 1, 4, 1), ("z", -1, 4, 1), ("vyf", 1, 1),
    ("vyf", -1, 1), ("z", 1, 2, 3), ("z", -1, 2, 3), ("po", 1, 1, 0), ("z", 1, 3, 2), ("z", -1, 3, 2), ("vyf", 1, 2),
    ("vyf", 1, -2), ("vyf", -1, 2), ("vyf", -1, -2), ("po", -1, -1, 0), ("vyf", 1, 3), ("vyf", 1, -3),
    ("vyf", -1, -3), ("z", 1, 1, 4), ("vyf", -1, 3), ("z", -1, 1, 4), ("po", 1, 1, 1), ("z", 1, 3, 3),
    ("z", -1, 3, 3), ("po", -1, -1, 1), ("xo", 1, -1, 0), ("xo", -1, 1, 0), ("xo", 1, -1, 1), ("xo", -1, 1, 1),
    ("xo", 1, -1, 2), ("xo", -1, 1, 2), ("xo", 1, -1, 3), ("xo", -1, 1, 3), ("vk", 0, 0, 0), ("xf", 1, 1, 0),
    ("xf", -1, -1, 0), ("xf", 1, 1, 1), ("xf", -1, -1, 1), ("vk", 0, 0, 1), ("vk", 1, 1, 0), ("vk", 1, -1, 0),
    ("xf", 1, 1, 2), ("xf", -1, -1, 2), ("xf", 1, 1, 3), ("xf", -1, -1, 3), ("vk", 0, 0, 2), ("vk", 1, 1, 1),
    ("vk", 1, -1, 1), ("vk", 2, 1, 0), ("vk", 2, -1, 0), ("vk", 0, 0, 3), ("vk", 1, 1, 2), ("vk", 1, -1, 2),
    ("vk", 1, 1, 3), ("vk", 1, -1, 3), ("vk", 2, 1, 1), ("vk", 2, -1, 1), ("vk", 2, 1, 2), ("vk", 2, -1, 2),
    ("vk", 2, 1, 3), ("vk", 2, -1, 3), ("vk", 0, 0, -1), ("vk", 1, 1, -1), ("vk", 1, -1, -1), ("vk", 2, 1, -1),
    ("vk", 2, -1, -1), ("vk", 0, 0, -2), ("vk", 1, 1, -2), ("vk", 1, -1, -2), ("vk", 2, 1, -2), ("vk", 2, -1, -2),
    ("vk", 0, 0, -3), ("vk", 1, 1, -3), ("vk", 1, -1, -3), ("vk", 2, -1, -3), ("vk", 2, 1, -3), ("C", "oc", 0, 0),
    ("z", 1, 1, 5), ("z", -1, 1, 5), ("C", "oc", 0, 1), ("C", "oc", 1, 0), ("z", 1, 4, 2), ("z", -1, 4, 2),
    ("C", "oc", 1, 1), ("z", 1, 2, 4), ("z", -1, 2, 4), ("C", "oc", 2, 0), ("z", 1, 4, 3), ("C", "oc", 2, 1),
    ("z", -1, 4, 3), ("C", "oc", 3, 0), ("z", 1, 2, 5), ("z", -1, 2, 5), ("po", 1, 1, 2), ("C", "oc", 3, 1),
    ("C", "oc", 4, 0), ("z", 1, 3, 4), ("z", -1, 3, 4), ("po", -1, -1, 2), ("C", "oc", 4, 1), ("z", 1, 1, 6),
    ("z", -1, 1, 6), ("po", 1, 1, 3), ("C", "oc", 5, 0), ("C", "oc", 5, 1), ("z", 1, 3, 5), ("z", -1, 3, 5),
    ("po", -1, -1, 3), ("C", "oc", 6, 0), ("z", 1, 1, 7), ("z", -1, 1, 7), ("C", "oc", 6, 1), ("z", 1, 4, 4),
    ("C", "oc", 7, 0), ("z", -1, 4, 4), ("C", "oc", 7, 1), ("z", 1, 2, 6), ("z", -1, 2, 6), ("po", -1, 1, 0),
    ("po", -1, 1, 1), ("C", "p3", 0, 0), ("C", "p3", 0, 1), ("z", 1, 4, 5), ("z", -1, 4, 5), ("po", 1, 1, 4),
    ("po", 1, -1, 0), ("po", 1, -1, 1), ("C", "p3", 4, 0), ("z", 1, 2, 7), ("C", "p3", 4, 1), ("z", -1, 2, 7),
    ("po", -1, -1, 4), ("po", -1, 1, 2), ("po", -1, 1, 3), ("C", "p3", 1, 0), ("z", 1, 3, 6), ("z", -1, 3, 6),
    ("po", 1, 1, 5), ("C", "p3", 1, 1), ("po", 1, -1, 2), ("po", 1, -1, 3), ("C", "p3", 5, 0), ("po", -1, -1, 5),
    ("z", 1, 3, 7), ("C", "p3", 5, 1), ("z", -1, 3, 7), ("po", -1, 1, 4), ("po", -1, 1, 5), ("C", "p3", 2, 0),
    ("z", 1, 4, 6), ("C", "p3", 2, 1), ("z", -1, 4, 6), ("po", 1, -1, 4), ("po", 1, -1, 5), ("C", "p3", 6, 0),
    ("C", "p3", 6, 1), ("z", 1, 4, 7), ("z", -1, 4, 7), ("pf", 1, 1, 0), ("pf", 1, 1, 1), ("C", "pl", 0, 0),
    ("po", 1, 1, 6), ("pf", -1, -1, 0), ("pf", -1, -1, 1), ("C", "pl", 4, 0), ("pf", 1, 1, 2), ("pf", 1, 1, 3),
    ("C", "pl", 1, 0), ("po", -1, -1, 6), ("pf", -1, -1, 2), ("pf", -1, -1, 3), ("C", "pl", 5, 0), ("pf", 1, 1, 4),
    ("pf", 1, 1, 5), ("C", "pl", 2, 0), ("pf", -1, -1, 4), ("pf", -1, -1, 5), ("C", "pl", 6, 0), ("po", 1, 1, 7),
    ("po", -1, 1, 6), ("po", -1, 1, 7), ("C", "p3", 3, 0), ("po", -1, -1, 7), ("C", "p3", 3, 1), ("po", 1, -1, 6),
    ("po", 1, -1, 7), ("C", "p3", 7, 0), ("C", "p3", 7, 1), ("pf", 1, 1, 6), ("pf", 1, 1, 7), ("C", "pl", 3, 0),
    ("pf", -1, -1, 6), ("pf", -1, -1, 7), ("C", "pl", 7, 0),
]


def starts():
    out = [(d, ("vz", d, 1)) for d in (1, -1)]
    out += [(None, ("z", d, 1, j)) for j in range(FIRST) for d in (1, -1)]
    out += [(None, ("vy", d, 0)) for d in (1, -1)]
    out.append((None, ("vk", 0, 0, 0)))
    return out


def follows(event):
    kind, out = event[0], []
    if kind == "xo":
        d, half, i = event[1:]
        if half == d:
            out.append((None, ("xf", d, d, i)))
    if kind == "z":
        d, h, j = event[1:]
        if h < HOPS:
            out.append((None, ("z", d, h + 1, j)))
        if h == ZNEXT and FIRST <= j + LAG < len(ZROWS):
            out.append((None, ("z", d, 1, j + LAG)))
        if h == HOPS:
            out += [(None, ("po", 1, d, j)), (None, ("po", -1, d, j))]
    if kind == "po":
        d, half, j = event[1:]
        if half == d:
            out.append((None, ("pf", d, d, j)))
    if kind == "vz":
        d, q = event[1:]
        if q < 3:
            out.append((d, ("vz", d, q + 1)))
        out += [(None, ("vy", 1, -d * q)), (None, ("vy", -1, -d * q))]
        out.append((None, ("vk", 0, 0, -d * q)))
    if kind == "vy":
        d, o = event[1:]
        out += [(None, ("vyf", d, o)), (None, ("vk", 1, d, o))]
    if kind == "vyf":
        d, o = event[1:]
        out.append((None, ("vk", 2, d, o)))
    return out


def offset(event):
    kind = event[0]
    if kind == "vz":
        return -event[1] * event[2]
    if kind in ("vy", "vyf"):
        return event[2]
    return event[3] if kind == "vk" else 0


def rows_of(half, pieces, i):
    return pl.ds((0 if half > 0 else 512) + sum(pieces[:i]), pieces[i])


SEMS = {
    "xo": (2, 2, len(XROWS)),
    "xf": (2, len(XROWS)),
    "z": (2, HOPS, len(ZROWS)),
    "po": (2, 2, len(ZROWS)),
    "pf": (2, len(ZROWS)),
    "vz": (2, 3),
    "vy": (2, 7),
    "vyf": (2, 7),
    "vk": (3, 2, 7),
}
KINDS = list(SEMS)


def sem_of(event):
    kind = event[0]
    way = lambda d: 0 if d > 0 else 1
    if kind in ("xo", "po"):
        return way(event[1]), way(event[2]), event[3]
    if kind in ("xf", "pf"):
        return way(event[1]), event[3]
    if kind == "z":
        return way(event[1]), event[2] - 1, event[3]
    if kind == "vz":
        return way(event[1]), event[2] - 1
    if kind in ("vy", "vyf"):
        return way(event[1]), event[2] + 3
    return event[1], way(event[2]), event[3] + 3


def kernel(
    a_in, v_in, res_in, a_mask_in, v_mask_in, r_mask_in, out,
    a, v, res, relay, a_mask, v_mask, r_mask, load_sem, a_sem, *sems
):
    recv = dict(zip(KINDS, sems[: len(KINDS)]))
    sent = dict(zip(KINDS, sems[len(KINDS) :]))
    row, col = lax.axis_index("row"), lax.axis_index("col")
    zh, x = row // 4, row % 4
    zl, y, k = col // 8, (col // 2) % 4, col % 2
    z = 4 * zh + zl

    def at(dx=0, dy=0, dz=0, other=False):
        znew = (z + dz + 8) % 8
        return (
            4 * (znew // 4) + (x + dx + 4) % 4,
            8 * (znew % 4) + 2 * ((y + dy + 4) % 4) + (1 - k if other else k),
        )

    mine = lambda dx: 4 * zh + (x + dx + 4) % 4
    theirs = lambda dx: 4 * (1 - zh) + (x + dx + 4) % 4

    def v_rows(o, dy, half=0):
        start = (8 * (zl + o) + 2 * ((y + dy + 4) % 4) + k) * TILE
        if half == 0:
            return v.at[pl.ds(pl.multiple_of(start, TILE), TILE)]
        start = start + (0 if half > 0 else TILE // 2)
        return v.at[pl.ds(pl.multiple_of(start, TILE // 2), TILE // 2)]

    def copy(event):
        kind = event[0]
        if kind in ("xo", "xf", "po", "pf"):
            d, half, i = event[1:]
            slot = (mine if kind[0] == "x" else theirs)(0 if kind[1] == "o" else -d)
            src = dst = a.at[slot, rows_of(half, XROWS if kind[0] == "x" else ZROWS, i)]
            to = at(dx=d)
        elif kind == "z":
            d, h, j = event[1:]
            rows = rows_of(d, ZROWS, j)
            src = a.at[mine(0), rows] if h == 1 else relay.at[h - 2, rows]
            if h < HOPS:
                dst = relay.at[h - 1, rows]
            else:
                dst = a.at[4 * (1 - ((z + ZSTEP * d + 8) % 8) // 4) + x, rows]
            to = at(dz=ZSTEP * d)
        elif kind == "vz":
            d, q = event[1:]
            src = dst = v_rows(-d * (q - 1), 0)
            to = at(dz=d)
        elif kind == "vy":
            d, o = event[1:]
            src = dst = v_rows(o, 0)
            to = at(dy=d)
        elif kind == "vyf":
            d, o = event[1:]
            src = dst = v_rows(o, -d, d)
            to = at(dy=d)
        else:
            via, d, o = event[1:]
            src = dst = v_rows(o, -d * via, d if via == 2 else 0)
            to = at(other=True)
        return pltpu.make_async_remote_copy(
            src_ref=src,
            dst_ref=dst,
            send_sem=sent[kind].at[sem_of(event)],
            recv_sem=recv[kind].at[sem_of(event)],
            device_id=to,
            device_id_type=MESH,
        )

    def within(o, act):
        if o == 0:
            act()
        else:
            pl.when((zl + o >= 0) & (zl + o <= 3))(act)

    copies = []

    def send(step, event):
        copies.append((event, step))
        go = lambda: copy(event).start()
        if step is None:
            go()
        else:
            within(step, go)

    def arrive(event):
        def act():
            copy(event).wait_recv()
            for step, then in follows(event):
                here = lambda then=then: copy(then).start()
                if step is None:
                    here()
                else:
                    within(step, here)

        within(offset(event), act)
        copies.extend((then, (offset(event), step)) for step, then in follows(event))

    def product(slots, rows, cols):
        total = None
        for slot in slots:
            part = jnp.dot(
                a[slot, rows, :],
                v[pl.ds(pl.multiple_of(slot * 512, 512), 512), cols],
                preferred_element_type=jnp.float32,
            )
            total = part if total is None else total + part
        return total

    def multiply(which, c, n):
        rows = pl.ds(c * MROWS[which], MROWS[which])
        cols = pl.ds(n * NCOLS[which], NCOLS[which])
        slots = {
            "oc": [mine(dx) for dx in (0, 1, 2, 3)],
            "p3": [theirs(dx) for dx in (0, 1, 3)],
            "pl": [theirs(2)],
        }[which]
        total = product(slots, rows, cols)
        if which == "oc":
            out[rows, cols] = total
        elif which == "p3":
            out[rows, cols] += total
        else:
            total = total + out[rows, cols]
            for i in range(MROWS[which] // TILE):
                for j in range(NCOLS[which] // TILE):
                    some = pl.ds(c * MROWS[which] + i * TILE, TILE)
                    tile = pl.ds(n * NCOLS[which] + j * TILE, TILE)
                    keep = r_mask[c * MROWS[which] // TILE + i, n * (NCOLS[which] // TILE) + j].astype(jnp.float32)
                    ladder = keep * total[i * TILE : (i + 1) * TILE, j * TILE : (j + 1) * TILE]
                    out[some, tile] = res[some, tile].astype(jnp.float32) + ladder

    own_a = mine(0)
    own_v = pl.ds(pl.multiple_of(col * TILE, TILE), TILE)
    loads = {
        "am": pltpu.make_async_copy(a_mask_in, a_mask, load_sem.at[0]),
        "vm": pltpu.make_async_copy(v_mask_in, v_mask, load_sem.at[1]),
        "v": pltpu.make_async_copy(v_in, v.at[own_v], load_sem.at[2]),
        "res": pltpu.make_async_copy(res_in, res, load_sem.at[3]),
        "rm": pltpu.make_async_copy(r_mask_in, r_mask, load_sem.at[4]),
    }
    for half in (1, -1):
        for i in range(len(XROWS)):
            rows = rows_of(half, XROWS, i)
            loads[half, i] = pltpu.make_async_copy(
                a_in.at[rows], a.at[own_a, rows], a_sem.at[0 if half > 0 else 1, i]
            )
    for load in loads.values():
        load.start()

    barrier = pltpu.get_barrier_semaphore()
    neighbours = [at(dx=1), at(dx=-1), at(dy=1), at(dy=-1), at(dz=1), at(dz=-1), at(other=True)]
    if ZSTEP > 1:
        neighbours += [at(dz=ZSTEP), at(dz=-ZSTEP)]
    for neighbour in neighbours:
        pl.semaphore_signal(barrier, inc=1, device_id=neighbour, device_id_type=MESH)

    loads["am"].wait()
    loads["vm"].wait()

    def screen_a(half, i):
        loads[half, i].wait()
        first = (0 if half > 0 else 512) + sum(XROWS[:i])
        for t in range(first // TILE, (first + XROWS[i]) // TILE):
            rows = pl.ds(t * TILE, TILE)
            for j in range(4):
                cols = pl.ds(j * TILE, TILE)
                keep = a_mask[j, t].astype(jnp.float32)
                a[own_a, rows, cols] = (a[own_a, rows, cols].astype(jnp.float32) * keep).astype(jnp.bfloat16)

    def screen_v():
        loads["v"].wait()
        for j in range(8):
            cols = pl.ds(j * TILE, TILE)
            keep = v_mask[0, j].astype(jnp.float32)
            v[own_v, cols] = (v[own_v, cols].astype(jnp.float32) * keep).astype(jnp.bfloat16)

    def start(step, event):
        go = lambda: copy(event).start()
        if step is None:
            go()
        else:
            within(step, go)
        copies.append((event, (0, step)))

    for i in range(len(XROWS)):
        for half in (1, -1):
            screen_a(half, i)
            if i == 0 and half == 1:
                pl.semaphore_wait(barrier, len(neighbours))
            start(None, ("xo", half, half, i))
        if i == 0:
            screen_v()
            for step, event in starts():
                start(step, event)
    for i in range(len(XROWS)):
        for d in (1, -1):
            start(None, ("xo", d, -d, i))

    loads["res"].wait()
    loads["rm"].wait()
    for op in ORDER:
        if op[0] == "C":
            multiply(*op[1:])
        else:
            arrive(op)

    for event, (o, step) in copies:
        def done(event=event, step=step):
            if step is None:
                copy(event).wait_send()
            else:
                within(step, lambda: copy(event).wait_send())

        within(o, done)


def write(held, out, sem):
    copies = [
        pltpu.make_async_copy(held.at[rows], out.at[rows], sem.at[i])
        for i, rows in enumerate(pl.ds(i * 256, 256) for i in range(4))
    ]
    for copy in copies:
        copy.start()
    for copy in copies:
        copy.wait()


def local(amplitudes, amplitude_mask, integrals, integral_mask, residual_in, residual_mask):
    hbm = pl.BlockSpec(memory_space=pltpu.HBM)
    vmem = pl.BlockSpec(memory_space=pltpu.VMEM)
    semaphores = [pltpu.SemaphoreType.DMA(shape) for shape in SEMS.values()]
    result = pl.pallas_call(
        kernel,
        out_shape=pltpu.VMEM((1024, 1024), jnp.float32),
        in_specs=[hbm] * 6,
        out_specs=vmem,
        scratch_shapes=[
            pltpu.VMEM((8, 1024, 512), jnp.bfloat16),
            pltpu.VMEM((4096, 1024), jnp.bfloat16),
            pltpu.VMEM((1024, 1024), jnp.bfloat16),
            pltpu.VMEM((HOPS - 1, 1024, 512), jnp.bfloat16),
            pltpu.SMEM((4, 8), jnp.int32),
            pltpu.SMEM((1, 8), jnp.int32),
            pltpu.SMEM((8, 8), jnp.int32),
            pltpu.SemaphoreType.DMA((5,)),
            pltpu.SemaphoreType.DMA((2, len(XROWS))),
            *semaphores,
            *semaphores,
        ],
        compiler_params=pltpu.CompilerParams(
            collective_id=0, has_side_effects=True, vmem_limit_bytes=60 * 1024 * 1024 - 65536
        ),
        cost_estimate=pl.CostEstimate(flops=2 * 1024 * 4096 * 1024, bytes_accessed=12 << 20, transcendentals=0),
        name="ladder",
    )(amplitudes, integrals, residual_in, amplitude_mask.T, integral_mask, residual_mask)
    return pl.pallas_call(
        write,
        out_shape=jax.ShapeDtypeStruct((1024, 1024), jnp.float32),
        in_specs=[vmem],
        out_specs=hbm,
        scratch_shapes=[pltpu.SemaphoreType.DMA((4,))],
        compiler_params=pltpu.CompilerParams(vmem_limit_bytes=16 * 1024 * 1024),
        name="write",
    )(result)


def solution(mesh):
    placed = P("col", "row")
    return jax.shard_map(
        local, mesh=mesh, in_specs=(placed,) * 6, out_specs=placed, check_vma=False
    )
```

time: 103 us -> 89.3 us (0.87)
  local copies, waits for them, and re-layouts: 10.6 us -> 0 us
  Pallas kernels: 92.5 us -> 88.8 us
    unnamed x12 -> x0, local copies, waits for them, and re-layouts: 10.6 us -> none
    pallas_call x1 -> x2, Pallas kernels: 92.5 us -> 88.8 us  [the longest x1 86.8 us: local(): pl.pallas_call(kernel, out_shape=pltpu.VMEM((1024, 1024), jnp.float32), i...]
where the time goes in v2:
time: 89.3 us; the launch traced here: 88.8 us
  Pallas kernels  88.8 us (99%)
    pallas_call x1, Pallas kernels, local(): pl.pallas_call(kernel, out_shape=pltpu.VMEM((1024, 1024), jnp.float32), i...  86.8 us
    pallas_call x1, Pallas kernels, local(): pl.pallas_call(write, out_shape=jax.ShapeDtypeStruct((1024, 1024), jnp.fl...  2.04 us

profile of v2, /device:TPU:6, one launch (start us, length us, event | category | flops | bytes accessed | tf_op | source)
XLA Modules:
  0.0 88.8 jit_solution(4850950279152890685)
XLA Ops:
  0.0 86.8 %ladder.1.held = f32[1024,1024]{1,0:T(8,128)S(1)} custom-call(bf16[1024,512]{1,0:T(8,128)(2,1)} %a_in.1, bf16[128,1024]{1,0:T(8,128)(2,1)} %v_in.1, bf16[1024,1024]{1,0:T(8,128)(2,1)} %res_in.1, s32[4,8]{1,0:T(4,128)} %bitcast.1, s32[1,8]{1,0:T(1,128)} %v_mask_in.1, s32[8,8]{1,0:T(8,128)} %r_mask_in.1), custom_call_target="tpu_custom_call" | custom-call | flops 8589934592 | bytes 12582912 | tf_op jit(solution)/shard_map/ladder/pallas_call | solution.py:383
  86.8 2.0 %write.1 = f32[1024,1024]{1,0:T(8,128)} custom-call(f32[1024,1024]{1,0:T(8,128)S(1)} %ladder.1.held), custom_call_target="tpu_custom_call" | custom-call | tf_op jit(solution)/shard_map/write/pallas_call | solution.py:407

commit v3 on v2

v3 whole, which is shorter than its diff:
```python
import functools

import jax
import jax.numpy as jnp
from jax import lax
from jax.experimental import pallas as pl
from jax.experimental.pallas import tpu as pltpu
from jax.sharding import PartitionSpec as P

MESH = pl.DeviceIdType.MESH
TILE = 128
XROWS = (128, 128, 128, 128)
ZROWS = (64, 64, 64, 64, 64, 64, 64, 64)
FIRST = 2
ZSTEP = 1
HOPS = 4 // ZSTEP

MROWS = {"oc": 128, "p3": 128, "pl": 128}
NCOLS = {"oc": 512, "p3": 512, "pl": 1024}

ORDER = [
    ("S", ("xo", -1, 1, 0)), ("vz", 1, 1), ("S", ("xo", -1, 1, 1)), ("vz", -1, 1), ("z", 1, 1, 0),
    ("S", ("xo", -1, 1, 2)), ("xo", 1, 1, 1), ("xo", 1, 1, 2), ("xo", -1, -1, 2), ("xo", -1, -1, 0), ("z", 1, 1, 1),
    ("vy", 1, 0), ("xo", 1, 1, 3), ("vz", 1, 2), ("z", -1, 1, 1), ("S", ("xo", 1, -1, 3)), ("z", 1, 2, 0),
    ("z", -1, 1, 0), ("xo", -1, -1, 3), ("vz", -1, 2), ("vy", -1, 0), ("z", -1, 2, 0), ("S", ("z", -1, 1, 2)),
    ("S", ("xo", 1, -1, 1)), ("vy", 1, 1), ("S", ("xo", 1, -1, 2)), ("xo", 1, 1, 0), ("S", ("xo", 1, -1, 0)),
    ("S", ("z", 1, 1, 2)), ("S", ("z", 1, 1, 3)), ("xo", -1, -1, 1), ("vz", 1, 3), ("vy", -1, -1), ("z", 1, 2, 1),
    ("z", -1, 2, 1), ("S", ("xo", -1, 1, 3)), ("S", ("z", -1, 1, 3)), ("vy", 1, -1), ("z", 1, 1, 2), ("vz", -1, 3),
    ("z", -1, 1, 2), ("z", 1, 3, 0), ("z", -1, 3, 1), ("vyf", 1, 0), ("vy", -1, 1), ("z", 1, 1, 3), ("z", -1, 1, 3),
    ("S", ("z", 1, 1, 4)), ("z", -1, 3, 0), ("S", ("z", -1, 1, 4)), ("z", 1, 2, 2), ("vy", 1, -3), ("vyf", 1, 1),
    ("vy", 1, 2), ("vy", -1, 2), ("S", ("z", 1, 1, 5)), ("vy", -1, -3), ("z", -1, 2, 2), ("vy", -1, 3),
    ("vy", -1, -2), ("vy", 1, -2), ("vyf", -1, 0), ("G", "xo", 1), ("z", 1, 4, 0), ("G", "xf"), ("z", 1, 3, 1),
    ("z", -1, 4, 0), ("S", ("z", -1, 1, 5)), ("G", "xo", -1), ("vy", 1, 3), ("z", -1, 4, 1), ("z", 1, 2, 3),
    ("z", -1, 2, 3), ("vyf", -1, -3), ("z", -1, 3, 2), ("vyf", 1, 2), ("z", -1, 1, 4), ("vyf", -1, -1),
    ("vyf", -1, 2), ("z", 1, 3, 2), ("vyf", 1, -3), ("z", 1, 4, 1), ("po", 1, 1, 0), ("z", 1, 1, 4), ("vyf", 1, -2),
    ("vyf", -1, -2), ("vyf", 1, 3), ("z", 1, 1, 5), ("vyf", -1, 1), ("po", -1, -1, 0), ("vyf", -1, 3),
    ("z", -1, 3, 3), ("vyf", 1, -1), ("z", -1, 4, 2), ("z", 1, 3, 3), ("z", 1, 4, 2), ("z", -1, 1, 5), ("G", "vk"),
    ("S", ("z", -1, 1, 6)), ("z", 1, 2, 4), ("C", "oc", 2, 1), ("C", "oc", 1, 1), ("C", "oc", 2, 0), ("z", -1, 2, 4),
    ("z", -1, 4, 3), ("S", ("z", 1, 1, 6)), ("C", "oc", 3, 0), ("C", "oc", 0, 1), ("z", 1, 2, 5), ("z", -1, 2, 5),
    ("S", ("z", 1, 1, 7)), ("C", "oc", 1, 0), ("z", 1, 4, 3), ("po", 1, 1, 2), ("C", "oc", 5, 0), ("po", -1, -1, 1),
    ("C", "oc", 6, 0), ("S", ("z", -1, 1, 7)), ("C", "oc", 3, 1), ("z", -1, 3, 4), ("po", 1, 1, 1), ("G", "po", 1, 0),
    ("po", -1, -1, 3), ("G", "po", -1, 0), ("z", 1, 3, 4), ("z", -1, 1, 6), ("C", "oc", 5, 1), ("z", 1, 1, 6),
    ("C", "oc", 7, 0), ("C", "oc", 4, 1), ("po", 1, 1, 3), ("C", "oc", 0, 0), ("z", 1, 1, 7), ("z", -1, 3, 5),
    ("po", -1, -1, 2), ("C", "oc", 6, 1), ("C", "oc", 4, 0), ("z", -1, 1, 7), ("z", 1, 4, 4), ("z", 1, 3, 5),
    ("C", "p3", 4, 1), ("G", "po", -1, 1), ("z", -1, 4, 4), ("z", -1, 2, 6), ("z", 1, 2, 6), ("C", "p3", 4, 0),
    ("z", -1, 4, 5), ("z", 1, 2, 7), ("G", "po", 1, 1), ("z", -1, 2, 7), ("z", 1, 4, 5), ("C", "p3", 0, 0),
    ("C", "p3", 1, 1), ("z", 1, 3, 6), ("C", "p3", 5, 1), ("po", 1, 1, 4), ("z", -1, 3, 6), ("G", "po", 1, 2),
    ("po", -1, -1, 5), ("C", "p3", 0, 1), ("G", "pf", 1, 0), ("po", -1, -1, 4), ("C", "p3", 6, 1), ("z", -1, 3, 7),
    ("po", 1, 1, 5), ("G", "po", -1, 2), ("C", "p3", 5, 0), ("z", 1, 3, 7), ("z", 1, 4, 6), ("z", -1, 4, 6),
    ("C", "p3", 1, 0), ("G", "pf", -1, 0), ("C", "pl", 0, 0), ("G", "pf", -1, 1), ("z", -1, 4, 7), ("G", "pf", -1, 2),
    ("z", 1, 4, 7), ("C", "oc", 7, 1), ("G", "pf", 1, 1), ("C", "pl", 1, 0), ("C", "p3", 6, 0), ("C", "p3", 2, 0),
    ("po", -1, -1, 6), ("C", "pl", 5, 0), ("po", 1, 1, 6), ("po", -1, -1, 7), ("C", "pl", 6, 0), ("po", 1, 1, 7),
    ("C", "p3", 2, 1), ("G", "po", -1, 3), ("G", "po", 1, 3), ("C", "p3", 3, 0), ("C", "pl", 4, 0), ("C", "p3", 3, 1),
    ("C", "p3", 7, 0), ("G", "pf", 1, 2), ("C", "pl", 2, 0), ("C", "p3", 7, 1), ("G", "pf", -1, 3), ("C", "pl", 7, 0),
    ("G", "pf", 1, 3), ("C", "pl", 3, 0),
]


def starts():
    out = [(d, ("vz", d, 1)) for d in (1, -1)]
    out += [(None, ("z", d, 1, j)) for j in range(FIRST) for d in (1, -1)]
    out += [(None, ("vy", d, 0)) for d in (1, -1)]
    out.append((None, ("vk", 0, 0, 0)))
    return out


def follows(event):
    kind, out = event[0], []
    if kind == "xo":
        d, half, i = event[1:]
        if half == d:
            out.append((None, ("xf", d, d, i)))
    if kind == "z":
        d, h, j = event[1:]
        if h < HOPS:
            out.append((None, ("z", d, h + 1, j)))
        if h == HOPS:
            out += [(None, ("po", 1, d, j)), (None, ("po", -1, d, j))]
    if kind == "po":
        d, half, j = event[1:]
        if half == d:
            out.append((None, ("pf", d, d, j)))
    if kind == "vz":
        d, q = event[1:]
        if q < 3:
            out.append((d, ("vz", d, q + 1)))
        out += [(None, ("vy", 1, -d * q)), (None, ("vy", -1, -d * q))]
        out.append((None, ("vk", 0, 0, -d * q)))
    if kind == "vy":
        d, o = event[1:]
        out += [(None, ("vyf", d, o)), (None, ("vk", 1, d, o))]
    if kind == "vyf":
        d, o = event[1:]
        out.append((None, ("vk", 2, d, o)))
    return out


def offset(event):
    kind = event[0]
    if kind == "vz":
        return -event[1] * event[2]
    if kind in ("vy", "vyf"):
        return event[2]
    return event[3] if kind == "vk" else 0


def rows_of(half, pieces, i):
    return pl.ds((0 if half > 0 else 512) + sum(pieces[:i]), pieces[i])


def way(d):
    return 0 if d > 0 else 1


def group_of(event):
    kind = event[0]
    if kind == "xo" and event[1] != event[2]:
        return ("xo", event[1])
    if kind in ("xf", "vk"):
        return (kind,)
    if kind == "pf" or kind == "po" and event[1] != event[2]:
        return (kind, event[1], sum(ZROWS[: event[3]]) // TILE)
    return None


RECV = {
    "xo": (2, len(XROWS)),
    "z": (2, HOPS, len(ZROWS)),
    "po": (2, len(ZROWS)),
    "vz": (4,),
    "vy": (2, 4),
    "vyf": (2, 4),
    "Gxo": (2,),
    "Gxf": (1,),
    "Gvk": (1,),
    "Gpo": (2, 4),
    "Gpf": (2, 4),
}
SENT = {"x": (2,), "z": (2,), "y": (2,), "vk": (1,), "vz": (2, 3)}


def kernel(
    a_in, v_in, res_in, a_mask_in, v_mask_in, r_mask_in, out,
    a, v, res, relay, a_mask, v_mask, r_mask, load_sem, a_sem, *sems
):
    recv = dict(zip(RECV, sems[: len(RECV)]))
    sent = dict(zip(SENT, sems[len(RECV) :]))
    row, col = lax.axis_index("row"), lax.axis_index("col")
    zh, x = row // 4, row % 4
    zl, y, k = col // 8, (col // 2) % 4, col % 2
    z = 4 * zh + zl

    def at(dx=0, dy=0, dz=0, other=False):
        znew = (z + dz + 8) % 8
        return (
            4 * (znew // 4) + (x + dx + 4) % 4,
            8 * (znew % 4) + 2 * ((y + dy + 4) % 4) + (1 - k if other else k),
        )

    mine = lambda dx: 4 * zh + (x + dx + 4) % 4
    theirs = lambda dx: 4 * (1 - zh) + (x + dx + 4) % 4

    def v_rows(o, dy, half=0):
        start = (8 * (zl + o) + 2 * ((y + dy + 4) % 4) + k) * TILE
        if half == 0:
            return v.at[pl.ds(pl.multiple_of(start, TILE), TILE)]
        start = start + (0 if half > 0 else TILE // 2)
        return v.at[pl.ds(pl.multiple_of(start, TILE // 2), TILE // 2)]

    def copy(event, sending=True):
        kind = event[0]
        if kind in ("xo", "xf", "po", "pf"):
            d, half, i = event[1:]
            slot = (mine if kind[0] == "x" else theirs)(0 if kind[1] == "o" else -d)
            src = dst = a.at[slot, rows_of(half, XROWS if kind[0] == "x" else ZROWS, i)]
            to = at(dx=d)
        elif kind == "z":
            d, h, j = event[1:]
            rows = rows_of(d, ZROWS, j)
            src = a.at[mine(0), rows] if h == 1 else relay.at[max(h - 2, 0), rows]
            if h < HOPS:
                dst = relay.at[h - 1, rows]
            else:
                dst = a.at[4 * (1 - ((z + ZSTEP * d + 8) % 8) // 4) + x, rows]
            to = at(dz=ZSTEP * d)
        elif kind == "vz":
            d, q = event[1:]
            src = dst = v_rows(-d * (q - 1), 0)
            to = at(dz=d)
        elif kind == "vy":
            d, o = event[1:]
            src = dst = v_rows(o, 0)
            to = at(dy=d)
        elif kind == "vyf":
            d, o = event[1:]
            src = dst = v_rows(o, -d, d)
            to = at(dy=d)
        else:
            via, d, o = event[1:]
            src = dst = v_rows(o, -d * via, d if via == 2 else 0)
            to = at(other=True)
        arrived = recv_sem(event)
        if kind == "vz":
            arrived = arrived[0 if sending else 1]
        return remote(src, dst, sent_sem(event), arrived, to)

    def remote(src, dst, send_sem, recv_sem, to):
        return pltpu.make_async_remote_copy(
            src_ref=src, dst_ref=dst, send_sem=send_sem, recv_sem=recv_sem, device_id=to, device_id_type=MESH
        )

    def sent_sem(event):
        kind = event[0]
        if kind == "vk":
            return sent["vk"].at[0]
        if kind == "vz":
            return sent["vz"].at[way(event[1]), event[2] - 1]
        return sent["z" if kind == "z" else "y" if kind[0] == "v" else "x"].at[way(event[1])]

    def recv_sem(event):
        kind, group = event[0], group_of(event)
        if group is not None:
            return recv["G" + kind].at[tuple([way(group[1]), *group[2:]] if len(group) > 1 else [0])]
        if kind in ("xo", "po"):
            return recv[kind].at[way(event[1]), event[3]]
        if kind == "z":
            return recv[kind].at[way(event[1]), event[2] - 1, event[3]]
        if kind == "vz":
            return recv[kind].at[zl - event[1] * (event[2] - 1)], recv[kind].at[zl - event[1] * event[2]]
        return recv[kind].at[way(event[1]), zl + event[2]]

    def within(o, act):
        if o == 0:
            act()
        else:
            pl.when((zl + o >= 0) & (zl + o <= 3))(act)

    def start(step, event):
        go = lambda: copy(event).start()
        if step is None:
            go()
        else:
            within(step, go)

    def arrive(event):
        def act():
            copy(event, sending=False).wait_recv()
            for step, then in follows(event):
                start(step, then)

        within(offset(event), act)

    def arrive_group(kind, d=1, c=0):
        if kind == "xo":
            rows, slot = pl.ds(0 if d < 0 else 512, 512), mine(-d)
        elif kind == "xf":
            rows, slot = pl.ds(0, 1024), mine(2)
        elif kind == "po":
            rows, slot = pl.ds((0 if d < 0 else 512) + c * TILE, TILE), theirs(-d)
        elif kind == "pf":
            rows, slot = pl.ds((0 if d > 0 else 512) + c * TILE, TILE), theirs(2)
        held = v.at[pl.ds(0, 2048)] if kind == "vk" else a.at[slot, rows]
        sem = recv["G" + kind].at[tuple([way(d), c][: len(RECV["G" + kind])])]
        remote(held, held, sent["vk"].at[0], sem, at(other=True)).wait_recv()

    def departures():
        for d in (1, -1):
            for kind, held in (("x", a.at[pl.ds(0, 3)]), ("z", a.at[pl.ds(0, HOPS), pl.ds(0, 512)]), ("y", v.at[pl.ds(0, 768)])):
                remote(held, held, sent[kind].at[way(d)], recv["Gvk"].at[0], at(other=True)).wait_send()
            for q in (1, 2, 3):
                leave = lambda: copy(("vz", d, q)).wait_send()
                within(d, lambda: within(-d * (q - 1), leave))
        held = v.at[pl.ds(0, 2048)]
        remote(held, held, sent["vk"].at[0], recv["Gvk"].at[0], at(other=True)).wait_send()

    def product(slots, rows, cols):
        total = None
        for slot in slots:
            part = jnp.dot(
                a[slot, rows, :],
                v[pl.ds(pl.multiple_of(slot * 512, 512), 512), cols],
                preferred_element_type=jnp.float32,
            )
            total = part if total is None else total + part
        return total

    def multiply(which, c, n):
        rows = pl.ds(c * MROWS[which], MROWS[which])
        cols = pl.ds(n * NCOLS[which], NCOLS[which])
        slots = {
            "oc": [mine(dx) for dx in (0, 1, 2, 3)],
            "p3": [theirs(dx) for dx in (0, 1, 3)],
            "pl": [theirs(2)],
        }[which]
        total = product(slots, rows, cols)
        if which == "oc":
            out[rows, cols] = total
        elif which == "p3":
            out[rows, cols] += total
        else:
            total = total + out[rows, cols]
            for i in range(MROWS[which] // TILE):
                for j in range(NCOLS[which] // TILE):
                    some = pl.ds(c * MROWS[which] + i * TILE, TILE)
                    tile = pl.ds(n * NCOLS[which] + j * TILE, TILE)
                    keep = r_mask[c * MROWS[which] // TILE + i, n * (NCOLS[which] // TILE) + j].astype(jnp.float32)
                    ladder = keep * total[i * TILE : (i + 1) * TILE, j * TILE : (j + 1) * TILE]
                    out[some, tile] = res[some, tile].astype(jnp.float32) + ladder

    own_a = mine(0)
    own_v = pl.ds(pl.multiple_of(col * TILE, TILE), TILE)
    loads = {
        "am": pltpu.make_async_copy(a_mask_in, a_mask, load_sem.at[0]),
        "vm": pltpu.make_async_copy(v_mask_in, v_mask, load_sem.at[1]),
        "v": pltpu.make_async_copy(v_in, v.at[own_v], load_sem.at[2]),
        "res": pltpu.make_async_copy(res_in, res, load_sem.at[3]),
        "rm": pltpu.make_async_copy(r_mask_in, r_mask, load_sem.at[4]),
    }
    for half in (1, -1):
        for i in range(len(XROWS)):
            rows = rows_of(half, XROWS, i)
            loads[half, i] = pltpu.make_async_copy(
                a_in.at[rows], a.at[own_a, rows], a_sem.at[0 if half > 0 else 1, i]
            )
    for load in loads.values():
        load.start()

    barrier = pltpu.get_barrier_semaphore()
    neighbours = [at(dx=1), at(dx=-1), at(dy=1), at(dy=-1), at(dz=1), at(dz=-1), at(other=True)]
    if ZSTEP > 1:
        neighbours += [at(dz=ZSTEP), at(dz=-ZSTEP)]
    for neighbour in neighbours:
        pl.semaphore_signal(barrier, inc=1, device_id=neighbour, device_id_type=MESH)

    loads["am"].wait()
    loads["vm"].wait()

    def screen_a(half, i):
        loads[half, i].wait()
        first = (0 if half > 0 else 512) + sum(XROWS[:i])
        for t in range(first // TILE, (first + XROWS[i]) // TILE):
            rows = pl.ds(t * TILE, TILE)
            for j in range(4):
                cols = pl.ds(j * TILE, TILE)
                keep = a_mask[j, t].astype(jnp.float32)
                a[own_a, rows, cols] = (a[own_a, rows, cols].astype(jnp.float32) * keep).astype(jnp.bfloat16)

    def screen_v():
        loads["v"].wait()
        for j in range(8):
            cols = pl.ds(j * TILE, TILE)
            keep = v_mask[0, j].astype(jnp.float32)
            v[own_v, cols] = (v[own_v, cols].astype(jnp.float32) * keep).astype(jnp.bfloat16)

    for i in range(len(XROWS)):
        for half in (1, -1):
            screen_a(half, i)
            if i == 0 and half == 1:
                pl.semaphore_wait(barrier, len(neighbours))
            start(None, ("xo", half, half, i))
        if i == 0:
            screen_v()
            for step, event in starts():
                start(step, event)
    loads["res"].wait()
    loads["rm"].wait()
    for op in ORDER:
        if op[0] == "C":
            multiply(*op[1:])
        elif op[0] == "G":
            arrive_group(*op[1:])
        elif op[0] == "S":
            start(None, op[1])
        else:
            arrive(op)
    departures()


def write(held, out, sem):
    copies = [
        pltpu.make_async_copy(held.at[rows], out.at[rows], sem.at[i])
        for i, rows in enumerate(pl.ds(i * 256, 256) for i in range(4))
    ]
    for copy in copies:
        copy.start()
    for copy in copies:
        copy.wait()


def local(amplitudes, amplitude_mask, integrals, integral_mask, residual_in, residual_mask):
    hbm = pl.BlockSpec(memory_space=pltpu.HBM)
    vmem = pl.BlockSpec(memory_space=pltpu.VMEM)
    semaphores = [pltpu.SemaphoreType.DMA(shape) for shape in [*RECV.values(), *SENT.values()]]
    result = pl.pallas_call(
        kernel,
        out_shape=pltpu.VMEM((1024, 1024), jnp.float32),
        in_specs=[hbm] * 6,
        out_specs=vmem,
        scratch_shapes=[
            pltpu.VMEM((8, 1024, 512), jnp.bfloat16),
            pltpu.VMEM((4096, 1024), jnp.bfloat16),
            pltpu.VMEM((1024, 1024), jnp.bfloat16),
            pltpu.VMEM((max(HOPS - 1, 1), 1024, 512), jnp.bfloat16),
            pltpu.SMEM((4, 8), jnp.int32),
            pltpu.SMEM((1, 8), jnp.int32),
            pltpu.SMEM((8, 8), jnp.int32),
            pltpu.SemaphoreType.DMA((5,)),
            pltpu.SemaphoreType.DMA((2, len(XROWS))),
            *semaphores,
        ],
        compiler_params=pltpu.CompilerParams(
            collective_id=0, has_side_effects=True, vmem_limit_bytes=60 * 1024 * 1024 - 65536
        ),
        cost_estimate=pl.CostEstimate(flops=2 * 1024 * 4096 * 1024, bytes_accessed=12 << 20, transcendentals=0),
        name="ladder",
    )(amplitudes, integrals, residual_in, amplitude_mask.T, integral_mask, residual_mask)
    return pl.pallas_call(
        write,
        out_shape=jax.ShapeDtypeStruct((1024, 1024), jnp.float32),
        in_specs=[vmem],
        out_specs=hbm,
        scratch_shapes=[pltpu.SemaphoreType.DMA((4,))],
        compiler_params=pltpu.CompilerParams(vmem_limit_bytes=16 * 1024 * 1024),
        name="write",
    )(result)


def solution(mesh):
    placed = P("col", "row")
    return jax.shard_map(
        local, mesh=mesh, in_specs=(placed,) * 6, out_specs=placed, check_vma=False
    )
```

time: 89.3 us -> 87.2 us (0.976); the launches traced: 88.8 us -> 85.6 us
  Pallas kernels: 88.8 us -> 85.6 us
    pallas_call x1, Pallas kernels: 86.8 us -> 83.5 us  [local(): pl.pallas_call(kernel, out_shape=pltpu.VMEM((1024, 1024), jnp.float32), i...]
where the time goes in v3:
time: 87.2 us; the launch traced here: 85.6 us
  Pallas kernels  85.6 us (98%)
    pallas_call x1, Pallas kernels, local(): pl.pallas_call(kernel, out_shape=pltpu.VMEM((1024, 1024), jnp.float32), i...  83.5 us
    pallas_call x1, Pallas kernels, local(): pl.pallas_call(write, out_shape=jax.ShapeDtypeStruct((1024, 1024), jnp.fl...  2.04 us

profile of v3, /device:TPU:6, one launch (start us, length us, event | category | flops | bytes accessed | tf_op | source)
XLA Modules:
  0.0 85.6 jit_solution(17941731962994144098)
XLA Ops:
  0.0 83.5 %ladder.1.held = f32[1024,1024]{1,0:T(8,128)S(1)} custom-call(bf16[1024,512]{1,0:T(8,128)(2,1)} %a_in.1, bf16[128,1024]{1,0:T(8,128)(2,1)} %v_in.1, bf16[1024,1024]{1,0:T(8,128)(2,1)} %res_in.1, s32[4,8]{1,0:T(4,128)} %bitcast.1, s32[1,8]{1,0:T(1,128)} %v_mask_in.1, s32[8,8]{1,0:T(8,128)} %r_mask_in.1), custom_call_target="tpu_custom_call" | custom-call | flops 8589934592 | bytes 12582912 | tf_op jit(solution)/shard_map/ladder/pallas_call | solution.py:394
  83.5 2.0 %write.1 = f32[1024,1024]{1,0:T(8,128)} custom-call(f32[1024,1024]{1,0:T(8,128)S(1)} %ladder.1.held), custom_call_target="tpu_custom_call" | custom-call | tf_op jit(solution)/shard_map/write/pallas_call | solution.py:417

commit v4 on v3

--- a/solution.py
+++ b/solution.py
@@ -11,48 +11,65 @@
 TILE = 128
 XROWS = (128, 128, 128, 128)
 ZROWS = (64, 64, 64, 64, 64, 64, 64, 64)
-FIRST = 2
+FIRST = 1
 ZSTEP = 1
 HOPS = 4 // ZSTEP
 
 MROWS = {"oc": 128, "p3": 128, "pl": 128}
 NCOLS = {"oc": 512, "p3": 512, "pl": 1024}
+LAST = (3, 7)
 
 ORDER = [
-    ("S", ("xo", -1, 1, 0)), ("vz", 1, 1), ("S", ("xo", -1, 1, 1)), ("vz", -1, 1), ("z", 1, 1, 0),
-    ("S", ("xo", -1, 1, 2)), ("xo", 1, 1, 1), ("xo", 1, 1, 2), ("xo", -1, -1, 2), ("xo", -1, -1, 0), ("z", 1, 1, 1),
-    ("vy", 1, 0), ("xo", 1, 1, 3), ("vz", 1, 2), ("z", -1, 1, 1), ("S", ("xo", 1, -1, 3)), ("z", 1, 2, 0),
-    ("z", -1, 1, 0), ("xo", -1, -1, 3), ("vz", -1, 2), ("vy", -1, 0), ("z", -1, 2, 0), ("S", ("z", -1, 1, 2)),
-    ("S", ("xo", 1, -1, 1)), ("vy", 1, 1), ("S", ("xo", 1, -1, 2)), ("xo", 1, 1, 0), ("S", ("xo", 1, -1, 0)),
-    ("S", ("z", 1, 1, 2)), ("S", ("z", 1, 1, 3)), ("xo", -1, -1, 1), ("vz", 1, 3), ("vy", -1, -1), ("z", 1, 2, 1),
-    ("z", -1, 2, 1), ("S", ("xo", -1, 1, 3)), ("S", ("z", -1, 1, 3)), ("vy", 1, -1), ("z", 1, 1, 2), ("vz", -1, 3),
-    ("z", -1, 1, 2), ("z", 1, 3, 0), ("z", -1, 3, 1), ("vyf", 1, 0), ("vy", -1, 1), ("z", 1, 1, 3), ("z", -1, 1, 3),
-    ("S", ("z", 1, 1, 4)), ("z", -1, 3, 0), ("S", ("z", -1, 1, 4)), ("z", 1, 2, 2), ("vy", 1, -3), ("vyf", 1, 1),
-    ("vy", 1, 2), ("vy", -1, 2), ("S", ("z", 1, 1, 5)), ("vy", -1, -3), ("z", -1, 2, 2), ("vy", -1, 3),
-    ("vy", -1, -2), ("vy", 1, -2), ("vyf", -1, 0), ("G", "xo", 1), ("z", 1, 4, 0), ("G", "xf"), ("z", 1, 3, 1),
-    ("z", -1, 4, 0), ("S", ("z", -1, 1, 5)), ("G", "xo", -1), ("vy", 1, 3), ("z", -1, 4, 1), ("z", 1, 2, 3),
-    ("z", -1, 2, 3), ("vyf", -1, -3), ("z", -1, 3, 2), ("vyf", 1, 2), ("z", -1, 1, 4), ("vyf", -1, -1),
-    ("vyf", -1, 2), ("z", 1, 3, 2), ("vyf", 1, -3), ("z", 1, 4, 1), ("po", 1, 1, 0), ("z", 1, 1, 4), ("vyf", 1, -2),
-    ("vyf", -1, -2), ("vyf", 1, 3), ("z", 1, 1, 5), ("vyf", -1, 1), ("po", -1, -1, 0), ("vyf", -1, 3),
-    ("z", -1, 3, 3), ("vyf", 1, -1), ("z", -1, 4, 2), ("z", 1, 3, 3), ("z", 1, 4, 2), ("z", -1, 1, 5), ("G", "vk"),
-    ("S", ("z", -1, 1, 6)), ("z", 1, 2, 4), ("C", "oc", 2, 1), ("C", "oc", 1, 1), ("C", "oc", 2, 0), ("z", -1, 2, 4),
-    ("z", -1, 4, 3), ("S", ("z", 1, 1, 6)), ("C", "oc", 3, 0), ("C", "oc", 0, 1), ("z", 1, 2, 5), ("z", -1, 2, 5),
-    ("S", ("z", 1, 1, 7)), ("C", "oc", 1, 0), ("z", 1, 4, 3), ("po", 1, 1, 2), ("C", "oc", 5, 0), ("po", -1, -1, 1),
-    ("C", "oc", 6, 0), ("S", ("z", -1, 1, 7)), ("C", "oc", 3, 1), ("z", -1, 3, 4), ("po", 1, 1, 1), ("G", "po", 1, 0),
-    ("po", -1, -1, 3), ("G", "po", -1, 0), ("z", 1, 3, 4), ("z", -1, 1, 6), ("C", "oc", 5, 1), ("z", 1, 1, 6),
-    ("C", "oc", 7, 0), ("C", "oc", 4, 1), ("po", 1, 1, 3), ("C", "oc", 0, 0), ("z", 1, 1, 7), ("z", -1, 3, 5),
-    ("po", -1, -1, 2), ("C", "oc", 6, 1), ("C", "oc", 4, 0), ("z", -1, 1, 7), ("z", 1, 4, 4), ("z", 1, 3, 5),
-    ("C", "p3", 4, 1), ("G", "po", -1, 1), ("z", -1, 4, 4), ("z", -1, 2, 6), ("z", 1, 2, 6), ("C", "p3", 4, 0),
-    ("z", -1, 4, 5), ("z", 1, 2, 7), ("G", "po", 1, 1), ("z", -1, 2, 7), ("z", 1, 4, 5), ("C", "p3", 0, 0),
-    ("C", "p3", 1, 1), ("z", 1, 3, 6), ("C", "p3", 5, 1), ("po", 1, 1, 4), ("z", -1, 3, 6), ("G", "po", 1, 2),
-    ("po", -1, -1, 5), ("C", "p3", 0, 1), ("G", "pf", 1, 0), ("po", -1, -1, 4), ("C", "p3", 6, 1), ("z", -1, 3, 7),
-    ("po", 1, 1, 5), ("G", "po", -1, 2), ("C", "p3", 5, 0), ("z", 1, 3, 7), ("z", 1, 4, 6), ("z", -1, 4, 6),
-    ("C", "p3", 1, 0), ("G", "pf", -1, 0), ("C", "pl", 0, 0), ("G", "pf", -1, 1), ("z", -1, 4, 7), ("G", "pf", -1, 2),
-    ("z", 1, 4, 7), ("C", "oc", 7, 1), ("G", "pf", 1, 1), ("C", "pl", 1, 0), ("C", "p3", 6, 0), ("C", "p3", 2, 0),
-    ("po", -1, -1, 6), ("C", "pl", 5, 0), ("po", 1, 1, 6), ("po", -1, -1, 7), ("C", "pl", 6, 0), ("po", 1, 1, 7),
-    ("C", "p3", 2, 1), ("G", "po", -1, 3), ("G", "po", 1, 3), ("C", "p3", 3, 0), ("C", "pl", 4, 0), ("C", "p3", 3, 1),
-    ("C", "p3", 7, 0), ("G", "pf", 1, 2), ("C", "pl", 2, 0), ("C", "p3", 7, 1), ("G", "pf", -1, 3), ("C", "pl", 7, 0),
-    ("G", "pf", 1, 3), ("C", "pl", 3, 0),
+    ("S", ("z", 1, 1, 1), 0), ("S", ("xo", -1, 1, 2)), ("S", ("z", -1, 1, 1), 2), ("S", ("z", -1, 1, 1), 1),
+    ("S", ("z", 1, 1, 1), 3), ("S", ("xo", 1, -1, 0)), ("S", ("z", 1, 1, 1), 2), ("S", ("z", 1, 1, 2), 0),
+    ("vz", 1, 1), ("S", ("z", 1, 1, 1), 1), ("S", ("z", -1, 1, 1), 0), ("vz", -1, 1), ("z", 1, 1, 0), ("xo", 1, 1, 1),
+    ("S", ("z", -1, 1, 2), 1), ("S", ("z", -1, 1, 3), 1), ("xo", 1, 1, 2), ("S", ("z", 1, 1, 2), 3),
+    ("S", ("xo", 1, -1, 2)), ("S", ("z", 1, 1, 3), 0), ("S", ("z", 1, 1, 2), 1), ("S", ("xo", -1, 1, 3)),
+    ("z", -1, 1, 1), ("S", ("xo", 1, -1, 1)), ("S", ("xo", -1, 1, 0)), ("S", ("z", -1, 1, 1), 3), ("z", -1, 1, 0),
+    ("vz", 1, 2), ("S", ("z", 1, 1, 4), 0), ("z", 1, 2, 0), ("vz", -1, 2), ("xo", -1, -1, 3),
+    ("S", ("z", 1, 1, 3), 3), ("z", -1, 2, 1), ("vy", -1, -1), ("S", ("z", 1, 1, 4), 3), ("vy", 1, 0),
+    ("xo", 1, 1, 0), ("S", ("z", -1, 1, 2), 2), ("z", 1, 1, 1), ("S", ("z", 1, 1, 2), 2), ("S", ("z", -1, 1, 3), 2),
+    ("S", ("z", -1, 1, 2), 0), ("S", ("z", -1, 1, 2), 3), ("vy", 1, 1), ("S", ("z", 1, 1, 3), 1),
+    ("S", ("xo", -1, 1, 1)), ("S", ("z", -1, 1, 3), 3), ("vy", -1, 0), ("S", ("z", -1, 1, 4), 1),
+    ("S", ("z", -1, 1, 3), 0), ("z", -1, 2, 0), ("xo", 1, 1, 3), ("S", ("z", 1, 1, 3), 2), ("xo", -1, -1, 1),
+    ("vz", 1, 3), ("S", ("z", -1, 1, 4), 0), ("xo", -1, -1, 0), ("vz", -1, 3), ("S", ("z", -1, 1, 4), 3),
+    ("S", ("z", 1, 1, 5), 0), ("z", 1, 2, 1), ("S", ("z", 1, 1, 5), 3), ("z", 1, 1, 2), ("S", ("z", 1, 1, 4), 2),
+    ("z", 1, 3, 0), ("vy", 1, 2), ("S", ("z", -1, 1, 5), 1), ("vy", 1, -2), ("S", ("z", -1, 1, 5), 3), ("vy", 1, -1),
+    ("S", ("z", 1, 1, 5), 2), ("S", ("z", 1, 1, 6), 0), ("xo", -1, -1, 2), ("S", ("z", -1, 1, 5), 0), ("z", -1, 1, 2),
+    ("z", -1, 3, 1), ("z", 1, 1, 3), ("S", ("z", 1, 1, 4), 1), ("z", 1, 3, 1), ("vy", -1, 1), ("z", -1, 1, 3),
+    ("z", -1, 2, 2), ("S", ("z", -1, 1, 4), 2), ("z", -1, 3, 0), ("vy", -1, -2), ("S", ("xo", 1, -1, 3)),
+    ("vy", -1, 3), ("S", ("z", 1, 1, 5), 1), ("z", -1, 4, 1), ("z", 1, 2, 2), ("z", -1, 2, 3), ("z", 1, 1, 4),
+    ("S", ("z", -1, 1, 6), 1), ("S", ("z", -1, 1, 6), 0), ("vyf", -1, 1), ("vyf", -1, 0), ("S", ("po", 1, -1, 1)),
+    ("vy", 1, 3), ("vy", -1, 2), ("vyf", -1, -1), ("vy", 1, -3), ("z", -1, 3, 2), ("vyf", 1, 0),
+    ("S", ("z", -1, 1, 6), 3), ("z", 1, 2, 3), ("vyf", -1, -2), ("S", ("z", -1, 1, 5), 2), ("vy", -1, -3),
+    ("z", 1, 4, 0), ("z", 1, 1, 5), ("z", -1, 4, 0), ("G", "xo", 1), ("z", 1, 4, 1), ("S", ("po", 1, -1, 0)),
+    ("z", -1, 3, 3), ("S", ("po", -1, 1, 1)), ("z", -1, 1, 4), ("vyf", -1, 3), ("S", ("z", 1, 1, 6), 1),
+    ("S", ("z", -1, 1, 7), 1), ("S", ("z", 1, 1, 7), 1), ("G", "xf"), ("S", ("po", -1, 1, 0)), ("z", 1, 3, 2),
+    ("S", ("z", 1, 1, 6), 3), ("vyf", 1, -2), ("S", ("z", -1, 1, 6), 2), ("G", "xo", -1), ("po", -1, -1, 0),
+    ("z", -1, 4, 2), ("po", 1, 1, 0), ("vyf", -1, -3), ("S", ("z", -1, 1, 7), 3), ("vyf", 1, -1), ("vyf", 1, 1),
+    ("S", ("po", 1, -1, 2)), ("po", -1, -1, 1), ("vyf", 1, 2), ("vyf", 1, -3), ("z", 1, 3, 3), ("z", 1, 2, 4),
+    ("vyf", 1, 3), ("z", -1, 1, 5), ("S", ("z", 1, 1, 6), 2), ("vyf", -1, 2), ("z", 1, 4, 2), ("z", -1, 2, 4),
+    ("G", "vk"), ("C", "oc", 2, 0), ("z", 1, 2, 5), ("z", -1, 4, 3), ("S", ("z", 1, 1, 7), 3),
+    ("S", ("z", -1, 1, 7), 2), ("z", 1, 4, 3), ("S", ("z", 1, 1, 7), 0), ("S", ("po", -1, 1, 2)),
+    ("S", ("z", -1, 1, 7), 0), ("S", ("po", -1, 1, 3)), ("G", "po", -1, 0), ("C", "oc", 2, 1), ("po", 1, 1, 1),
+    ("S", ("po", 1, -1, 3)), ("z", -1, 2, 5), ("C", "oc", 0, 0), ("po", -1, -1, 2), ("z", 1, 3, 4),
+    ("S", ("z", 1, 1, 7), 2), ("C", "oc", 1, 1), ("z", -1, 3, 4), ("G", "po", 1, 0), ("C", "oc", 0, 1),
+    ("z", -1, 1, 6), ("po", 1, 1, 3), ("z", 1, 1, 6), ("po", 1, 1, 2), ("C", "oc", 1, 0), ("po", -1, -1, 3),
+    ("z", -1, 1, 7), ("G", "pf", -1, 0), ("C", "oc", 6, 0), ("z", 1, 3, 5), ("C", "oc", 4, 0), ("z", -1, 3, 5),
+    ("C", "oc", 3, 0), ("G", "po", -1, 1), ("z", 1, 4, 4), ("C", "oc", 3, 1), ("z", -1, 4, 4), ("z", 1, 1, 7),
+    ("S", ("po", 1, -1, 4)), ("C", "oc", 7, 0), ("C", "oc", 5, 1), ("z", 1, 2, 6), ("S", ("po", -1, 1, 4)),
+    ("z", -1, 2, 6), ("z", 1, 4, 5), ("S", ("po", -1, 1, 5)), ("C", "p3", 1, 0), ("C", "oc", 4, 1), ("G", "pf", 1, 0),
+    ("z", 1, 2, 7), ("z", -1, 2, 7), ("z", -1, 4, 5), ("C", "oc", 5, 0), ("po", 1, 1, 4), ("C", "p3", 4, 1),
+    ("G", "pf", 1, 1), ("z", 1, 3, 6), ("po", -1, -1, 4), ("z", -1, 3, 6), ("S", ("po", 1, -1, 5)),
+    ("G", "po", -1, 2), ("G", "po", 1, 1), ("po", 1, 1, 5), ("z", -1, 3, 7), ("z", 1, 3, 7), ("po", -1, -1, 5),
+    ("C", "p3", 4, 0), ("z", 1, 4, 6), ("z", -1, 4, 6), ("S", ("po", -1, 1, 6)), ("C", "p3", 2, 1),
+    ("S", ("po", 1, -1, 6)), ("C", "oc", 7, 1), ("C", "p3", 2, 0), ("C", "p3", 0, 1), ("C", "p3", 1, 1),
+    ("z", -1, 4, 7), ("z", 1, 4, 7), ("S", ("po", 1, -1, 7)), ("C", "oc", 6, 1), ("po", 1, 1, 6), ("G", "pf", -1, 2),
+    ("G", "pf", -1, 1), ("S", ("po", -1, 1, 7)), ("C", "p3", 5, 1), ("C", "pl", 4, 0), ("G", "po", 1, 2),
+    ("C", "p3", 6, 0), ("C", "pl", 1, 0), ("C", "p3", 0, 0), ("po", -1, -1, 6), ("G", "pf", 1, 2), ("C", "p3", 5, 0),
+    ("po", 1, 1, 7), ("C", "pl", 2, 0), ("po", -1, -1, 7), ("C", "p3", 6, 1), ("G", "po", 1, 3), ("G", "po", -1, 3),
+    ("C", "p3", 3, 0), ("C", "p3", 7, 0), ("C", "p3", 3, 1), ("C", "pl", 0, 0), ("C", "p3", 7, 1), ("C", "pl", 5, 0),
+    ("C", "pl", 6, 0), ("G", "pf", 1, 3), ("G", "pf", -1, 3),
 ]
 
 
@@ -75,7 +92,7 @@
         if h < HOPS:
             out.append((None, ("z", d, h + 1, j)))
         if h == HOPS:
-            out += [(None, ("po", 1, d, j)), (None, ("po", -1, d, j))]
+            out.append((None, ("po", d, d, j)))
     if kind == "po":
         d, half, j = event[1:]
         if half == d:
@@ -140,8 +157,8 @@
 
 
 def kernel(
-    a_in, v_in, res_in, a_mask_in, v_mask_in, r_mask_in, out,
-    a, v, res, relay, a_mask, v_mask, r_mask, load_sem, a_sem, *sems
+    a_in, v_in, res_in, a_mask_in, v_mask_in, r_mask_in, out, a, v, keeps,
+    res, relay, a_mask, v_mask, r_mask, load_sem, a_sem, *sems
 ):
     recv = dict(zip(RECV, sems[: len(RECV)]))
     sent = dict(zip(SENT, sems[len(RECV) :]))
@@ -242,6 +259,13 @@
         else:
             within(step, go)
 
+    def send_own(event, place=None):
+        if place is None:
+            start(None, event)
+        else:
+            here = zl if event[1] > 0 else 3 - zl
+            pl.when(here == place)(lambda: start(None, event))
+
     def arrive(event):
         def act():
             copy(event, sending=False).wait_recv()
@@ -295,17 +319,17 @@
         total = product(slots, rows, cols)
         if which == "oc":
             out[rows, cols] = total
-        elif which == "p3":
+        elif which == "p3" and c not in LAST:
             out[rows, cols] += total
         else:
             total = total + out[rows, cols]
-            for i in range(MROWS[which] // TILE):
-                for j in range(NCOLS[which] // TILE):
-                    some = pl.ds(c * MROWS[which] + i * TILE, TILE)
-                    tile = pl.ds(n * NCOLS[which] + j * TILE, TILE)
-                    keep = r_mask[c * MROWS[which] // TILE + i, n * (NCOLS[which] // TILE) + j].astype(jnp.float32)
-                    ladder = keep * total[i * TILE : (i + 1) * TILE, j * TILE : (j + 1) * TILE]
-                    out[some, tile] = res[some, tile].astype(jnp.float32) + ladder
+            for j in range(NCOLS[which] // TILE):
+                at_tile = n * (NCOLS[which] // TILE) + j
+                tile = pl.ds(at_tile * TILE, TILE)
+                keep = r_mask[c, at_tile].astype(jnp.float32)
+                out[rows, tile] = res[rows, tile].astype(jnp.float32) + keep * total[:, j * TILE : (j + 1) * TILE]
+                if c in LAST:
+                    keeps[LAST.index(c), :, tile] = jnp.full((8, TILE), keep)
 
     own_a = mine(0)
     own_v = pl.ds(pl.multiple_of(col * TILE, TILE), TILE)
@@ -370,19 +394,25 @@
         elif op[0] == "G":
             arrive_group(*op[1:])
         elif op[0] == "S":
-            start(None, op[1])
+            send_own(*op[1:])
         else:
             arrive(op)
     departures()
 
 
-def write(held, out, sem):
-    copies = [
-        pltpu.make_async_copy(held.at[rows], out.at[rows], sem.at[i])
-        for i, rows in enumerate(pl.ds(i * 256, 256) for i in range(4))
-    ]
+def finish(held, a, v, keeps, out, last, sem):
+    spans = [pl.ds(0, 3 * TILE), pl.ds(4 * TILE, 3 * TILE)]
+    copies = [pltpu.make_async_copy(held.at[rows], out.at[rows], sem.at[i]) for i, rows in enumerate(spans)]
     for copy in copies:
         copy.start()
+    slot = 4 * (1 - lax.axis_index("row") // 4) + (lax.axis_index("row") + 2) % 4
+    for i, c in enumerate(LAST):
+        rows = pl.ds(c * TILE, TILE)
+        block = v[pl.ds(pl.multiple_of(slot * 512, 512), 512), :]
+        total = jnp.dot(a[slot, rows, :], block, preferred_element_type=jnp.float32)
+        last[i] = held[rows, :] + keeps[i, 0:1, :] * total
+        copies.append(pltpu.make_async_copy(last.at[i], out.at[rows], sem.at[2 + i]))
+        copies[-1].start()
     for copy in copies:
         copy.wait()
 
@@ -391,14 +421,17 @@
     hbm = pl.BlockSpec(memory_space=pltpu.HBM)
     vmem = pl.BlockSpec(memory_space=pltpu.VMEM)
     semaphores = [pltpu.SemaphoreType.DMA(shape) for shape in [*RECV.values(), *SENT.values()]]
-    result = pl.pallas_call(
+    held = pl.pallas_call(
         kernel,
-        out_shape=pltpu.VMEM((1024, 1024), jnp.float32),
-        in_specs=[hbm] * 6,
-        out_specs=vmem,
-        scratch_shapes=[
+        out_shape=[
+            pltpu.VMEM((1024, 1024), jnp.float32),
             pltpu.VMEM((8, 1024, 512), jnp.bfloat16),
             pltpu.VMEM((4096, 1024), jnp.bfloat16),
+            pltpu.VMEM((len(LAST), 8, 1024), jnp.float32),
+        ],
+        in_specs=[hbm] * 6,
+        out_specs=[vmem] * 4,
+        scratch_shapes=[
             pltpu.VMEM((1024, 1024), jnp.bfloat16),
             pltpu.VMEM((max(HOPS - 1, 1), 1024, 512), jnp.bfloat16),
             pltpu.SMEM((4, 8), jnp.int32),
@@ -409,20 +442,20 @@
             *semaphores,
         ],
         compiler_params=pltpu.CompilerParams(
-            collective_id=0, has_side_effects=True, vmem_limit_bytes=60 * 1024 * 1024 - 65536
+            collective_id=0, has_side_effects=True, vmem_limit_bytes=44 * 1024 * 1024 - 131072
         ),
         cost_estimate=pl.CostEstimate(flops=2 * 1024 * 4096 * 1024, bytes_accessed=12 << 20, transcendentals=0),
         name="ladder",
     )(amplitudes, integrals, residual_in, amplitude_mask.T, integral_mask, residual_mask)
     return pl.pallas_call(
-        write,
+        finish,
         out_shape=jax.ShapeDtypeStruct((1024, 1024), jnp.float32),
-        in_specs=[vmem],
+        in_specs=[vmem] * 4,
         out_specs=hbm,
-        scratch_shapes=[pltpu.SemaphoreType.DMA((4,))],
+        scratch_shapes=[pltpu.VMEM((len(LAST), TILE, 1024), jnp.float32), pltpu.SemaphoreType.DMA((2 + len(LAST),))],
         compiler_params=pltpu.CompilerParams(vmem_limit_bytes=16 * 1024 * 1024),
-        name="write",
-    )(result)
+        name="finish",
+    )(*held)
 
 
 def solution(mesh):

time: 87.2 us -> 86.3 us (0.990); the launches traced: 85.6 us -> 86.2 us
  no operation moved by 1% of the time
where the time goes in v4:
time: 86.3 us; the launch traced here: 86.2 us
  Pallas kernels  86.2 us (100%)
    pallas_call x1, Pallas kernels, local(): pl.pallas_call(kernel, out_shape=[pltpu.VMEM((1024, 1024), jnp.float32),...  84.2 us
    pallas_call x1, Pallas kernels, local(): pl.pallas_call(finish, out_shape=jax.ShapeDtypeStruct((1024, 1024), jnp.f...  2.06 us

profile of v4, /device:TPU:6, one launch (start us, length us, event | category | flops | bytes accessed | tf_op | source)
XLA Modules:
  0.0 86.2 jit_solution(1173739107210798395)
XLA Ops:
  0.0 84.2 %ladder.1 = (f32[1024,1024]{1,0:T(8,128)S(1)}, bf16[8,1024,512]{2,1,0:T(8,128)(2,1)S(1)}, bf16[4096,1024]{1,0:T(8,128)(2,1)S(1)}, f32[2,8,1024]{2,1,0:T(8,128)S(1)}) custom-call(bf16[1024,512]{1,0:T(8,128)(2,1)} %a_in.1, bf16[128,1024]{1,0:T(8,128)(2,1)} %v_in.1, bf16[1024,1024]{1,0:T(8,128)(2,1)} %res_in.1, s32[4,8]{1,0:T(4,128)} %bitcast.1, ...), custom_call_target="tpu_custom_call" | custom-call | flops 8589934592 | bytes 12582912 | tf_op jit(solution)/shard_map/ladder/pallas_call | solution.py:424
  84.2 2.1 %finish.1 = f32[1024,1024]{1,0:T(8,128)} custom-call(f32[1024,1024]{1,0:T(8,128)S(1)} %get-tuple-element.9.held, bf16[8,1024,512]{2,1,0:T(8,128)(2,1)S(1)} %get-tuple-element.10.a, bf16[4096,1024]{1,0:T(8,128)(2,1)S(1)} %get-tuple-element.11.v, f32[2,8,1024]{2,1,0:T(8,128)S(1)} %get-tuple-element.12.keeps), custom_call_target="tpu_custom_call" | custom-call | tf_op jit(solution)/shard_map/finish/pallas_call | solution.py:450

commit v5 on v4

--- a/solution.py
+++ b/solution.py
@@ -346,8 +346,10 @@
             loads[half, i] = pltpu.make_async_copy(
                 a_in.at[rows], a.at[own_a, rows], a_sem.at[0 if half > 0 else 1, i]
             )
-    for load in loads.values():
-        load.start()
+    order = ["am", (1, 0), (-1, 0), "vm", "v"]
+    order += [(half, i) for i in range(1, len(XROWS)) for half in (1, -1)] + ["rm", "res"]
+    for name in order:
+        loads[name].start()
 
     barrier = pltpu.get_barrier_semaphore()
     neighbours = [at(dx=1), at(dx=-1), at(dy=1), at(dy=-1), at(dz=1), at(dz=-1), at(other=True)]
@@ -386,9 +388,11 @@
             screen_v()
             for step, event in starts():
                 start(step, event)
-    loads["res"].wait()
-    loads["rm"].wait()
-    for op in ORDER:
+    first = ORDER.index(next(op for op in ORDER if op[0] == "C"))
+    for i, op in enumerate(ORDER):
+        if i == first:
+            loads["res"].wait()
+            loads["rm"].wait()
         if op[0] == "C":
             multiply(*op[1:])
         elif op[0] == "G":

time: 86.3 us -> 86.3 us (level)
  no operation moved by 1% of the time
where the time goes in v5:
time: 86.3 us; the launch traced here: 86.2 us
  Pallas kernels  86.2 us (100%)
    pallas_call x1, Pallas kernels, local(): pl.pallas_call(kernel, out_shape=[pltpu.VMEM((1024, 1024), jnp.float32),...  84.2 us
    pallas_call x1, Pallas kernels, local(): pl.pallas_call(finish, out_shape=jax.ShapeDtypeStruct((1024, 1024), jnp.f...  2.06 us

profile of v5, /device:TPU:6, one launch (start us, length us, event | category | flops | bytes accessed | tf_op | source)
XLA Modules:
  0.0 86.2 jit_solution(12912867701535872124)
XLA Ops:
  0.0 84.2 %ladder.1 = (f32[1024,1024]{1,0:T(8,128)S(1)}, bf16[8,1024,512]{2,1,0:T(8,128)(2,1)S(1)}, bf16[4096,1024]{1,0:T(8,128)(2,1)S(1)}, f32[2,8,1024]{2,1,0:T(8,128)S(1)}) custom-call(bf16[1024,512]{1,0:T(8,128)(2,1)} %a_in.1, bf16[128,1024]{1,0:T(8,128)(2,1)} %v_in.1, bf16[1024,1024]{1,0:T(8,128)(2,1)} %res_in.1, s32[4,8]{1,0:T(4,128)} %bitcast.1, ...), custom_call_target="tpu_custom_call" | custom-call | flops 8589934592 | bytes 12582912 | tf_op jit(solution)/shard_map/ladder/pallas_call | solution.py:428
  84.2 2.1 %finish.1 = f32[1024,1024]{1,0:T(8,128)} custom-call(f32[1024,1024]{1,0:T(8,128)S(1)} %get-tuple-element.9.held, bf16[8,1024,512]{2,1,0:T(8,128)(2,1)S(1)} %get-tuple-element.10.a, bf16[4096,1024]{1,0:T(8,128)(2,1)S(1)} %get-tuple-element.11.v, f32[2,8,1024]{2,1,0:T(8,128)S(1)} %get-tuple-element.12.keeps), custom_call_target="tpu_custom_call" | custom-call | tf_op jit(solution)/shard_map/finish/pallas_call | solution.py:454
